TPU v7x, 512 devices: a whole 4x8x8 slice. The times are simulated.
512 devices in a mesh: ctx: 64 (over y_hi, x, z), chan: 8 (over y_lo, core).
Axes of the slice: x: 4, y: 8 (y_hi: 2, y_lo: 4; y = y_hi * 4 + y_lo), z: 8, core: 2. Of those that a mesh axis runs over, the one named last changes fastest.
Arguments:
- gate_q: bfloat16 [16, 262144], P('chan', 'ctx'), may hold values from -6 to 6
- gate_k: bfloat16 [16, 262144], P('chan', 'ctx'), may hold values from -6 to 6
- values: bfloat16 [16, 262144], P('chan', 'ctx'), may hold values from -6 to 6
- filter_taps: float32 [262144], P('ctx'), may hold values from -6 to 6
- skip_gain: float32 [16], P('chan'), may hold values from 0.5 to 1.5
- cotangent: bfloat16 [16, 262144], P('chan', 'ctx'), may hold values from -6 to 6
Outputs:
- gated_output: bfloat16 [16, 262144], P('chan', 'ctx')
- grad_query: bfloat16 [16, 262144], P('chan', 'ctx')
- grad_key: bfloat16 [16, 262144], P('chan', 'ctx')
- grad_values: bfloat16 [16, 262144], P('chan', 'ctx')
- grad_filter: float32 [262144], P('ctx')
All inputs are finite; a program needn't handle non-finite values.
Results may differ from a plain program's by a relative error of at most 0.0024.
Values sent between devices are 32-bit elements; how exact they have to be, the bound alone decides.
No kernel may reach another device: no remote copies, remote signals or barrier semaphores. Data moves between devices by JAX's collectives and lax.ppermute only.
A program may use at most 64 MiB of HBM per device.

v0:
```python
import numpy as np

import jax
import jax.numpy as jnp
from jax import lax
from jax.experimental import pallas as pl
from jax.experimental.pallas import tpu as pltpu
from jax.sharding import PartitionSpec as P

BLOCK = 4096
BLOCKS = 64
ROWS = 32
LANES = 128
HALF = 64
SIGNALS = 5
WIDTH = SIGNALS * LANES


def split(value):
    high = value.astype(jnp.bfloat16)
    return high, (value - high.astype(jnp.float32)).astype(jnp.bfloat16)


def split_table(table):
    high = table.astype(np.float32).astype(jnp.bfloat16)
    low = (table - high.astype(np.float64)).astype(np.float32).astype(jnp.bfloat16)
    return high, low


def make_tables():
    a = np.arange(ROWS)
    b = np.arange(LANES)
    first = np.exp(-2j * np.pi * (a[:, None] * a[None, :] / ROWS + LANES * a[None, :] / (4 * BLOCK)))
    high, low = split_table(np.concatenate([first.real, first.imag], 0))
    first_table = np.concatenate([high, low, high], 1)
    last = np.conj(first.T) / BLOCK / (BLOCK * BLOCKS) ** 0.5
    high, low = split_table(np.concatenate([last.real, -last.imag], 1))
    last_table = np.concatenate([high, low, high], 1)
    twiddle = np.exp(-2j * np.pi * b[None, :] * (4 * a[:, None] + 1) / (4 * BLOCK))
    twiddle = np.stack([twiddle.real, twiddle.imag]).astype(np.float32)
    angle = 2 * np.pi * (b[:, None] * b[None, :] % LANES) / LANES
    cos, sin = np.cos(angle), np.sin(angle)
    real = np.concatenate([cos, sin], 0)
    imag = np.concatenate([-sin, cos], 0)
    order = [real[:, :HALF], imag[:, :HALF], real[:, HALF:], imag[:, HALF:]]
    second = np.concatenate(order, 1)
    return first_table, last_table, twiddle, split_table(second), split_table(second.T)


def dot(left, right):
    return jnp.dot(left, right, preferred_element_type=jnp.float32)


def dot3(value, high, low):
    value_high, value_low = split(value)
    return dot(value_high, high) + (dot(value_high, low) + dot(value_low, high))


def forward_kernel(
    key_ref, values_ref, cot_ref, query_ref, taps_ref, first_ref, twiddle_ref, high_ref, low_ref, out_ref, rows_ref
):
    f32 = jnp.float32
    mixed = key_ref[...].astype(f32) * values_ref[...].astype(f32)
    grad = cot_ref[...].astype(f32) * query_ref[...].astype(f32)
    for j in range(ROWS):
        cols = slice(LANES * j, LANES * (j + 1))
        rows_ref[0:2, j, :] = mixed[:, cols]
        rows_ref[2:4, j, :] = grad[:, cols]
    signals = [rows_ref[s] for s in range(4)] + [taps_ref[...]]
    high, low = split(jnp.concatenate(signals, 1))
    spread = dot(first_ref[...], jnp.concatenate([high, high, low], 0))
    tw_re, tw_im = twiddle_ref[0], twiddle_ref[1]
    turned = []
    for s in range(SIGNALS):
        cols = slice(LANES * s, LANES * (s + 1))
        re, im = spread[:ROWS, cols], spread[ROWS:, cols]
        turned.append(jnp.concatenate([re * tw_re - im * tw_im, re * tw_im + im * tw_re], 1))
    spectra = dot3(jnp.concatenate(turned, 0), high_ref[...], low_ref[...])
    for s in range(SIGNALS):
        for h in range(2):
            out_ref[ROWS * h : ROWS * (h + 1), 0, LANES * s : LANES * (s + 1)] = spectra[
                ROWS * s : ROWS * (s + 1), LANES * h : LANES * (h + 1)
            ]


def blocks_kernel(in_ref, out_ref, past_ref, next_ref, coef_ref, corr_ref):
    real_lane = lax.broadcasted_iota(jnp.int32, (BLOCKS, LANES), 1) < HALF
    zeros = jnp.zeros((BLOCKS, LANES), jnp.float32)

    def signal(s):
        return in_ref[:, 0, LANES * s : LANES * (s + 1)]

    def swap(value):
        return pltpu.roll(value, HALF, 1)

    taps = signal(4)
    corr_ref[0:8] = zeros[:8]
    corr_ref[8:72] = taps
    before = swap(corr_ref[7:71])
    taps = taps + jnp.where(real_lane, -before, before)
    swapped = swap(taps)
    coef_ref[0] = jnp.where(real_lane, taps, swapped)
    coef_ref[1] = jnp.where(real_lane, -swapped, taps)
    for c in range(2):
        mixed, grad = signal(c), signal(2 + c)
        mixed_swap = swap(mixed)
        past_ref[2 * c, 0:BLOCKS] = zeros
        past_ref[2 * c, BLOCKS:] = mixed
        past_ref[2 * c + 1, 0:BLOCKS] = zeros
        past_ref[2 * c + 1, BLOCKS:] = mixed_swap
        next_ref[2 * c, 0:BLOCKS] = grad
        next_ref[2 * c, BLOCKS:] = zeros
        next_ref[2 * c + 1, 0:BLOCKS] = swap(grad)
        next_ref[2 * c + 1, BLOCKS:] = zeros
        coef_ref[2 + 2 * c] = jnp.where(real_lane, mixed, mixed_swap)
        coef_ref[3 + 2 * c] = jnp.where(real_lane, mixed_swap, -mixed)

    for r in range(BLOCKS // 8):
        rows = slice(8 * r, 8 * r + 8)
        conv0 = conv1 = jnp.zeros((8, LANES), jnp.float32)
        for j in range(8 * r + 8):
            window = slice(BLOCKS + 8 * r - j, BLOCKS + 8 * r - j + 8)
            fa, fb = coef_ref[0, j : j + 1, :], coef_ref[1, j : j + 1, :]
            conv0 += fa * past_ref[0, window, :] + fb * past_ref[1, window, :]
            conv1 += fa * past_ref[2, window, :] + fb * past_ref[3, window, :]
        out_ref[rows, 0, 0:LANES] = conv0
        out_ref[rows, 0, LANES : 2 * LANES] = conv1
        grad0 = grad1 = corr = jnp.zeros((8, LANES), jnp.float32)
        for j in range(BLOCKS - 8 * r):
            window = slice(8 * r + j, 8 * r + j + 8)
            fa, fb = coef_ref[0, j : j + 1, :], coef_ref[1, j : j + 1, :]
            g0, g0s = next_ref[0, window, :], next_ref[1, window, :]
            g1, g1s = next_ref[2, window, :], next_ref[3, window, :]
            grad0 += fa * g0 - fb * g0s
            grad1 += fa * g1 - fb * g1s
            corr += coef_ref[2, j : j + 1, :] * g0 + coef_ref[3, j : j + 1, :] * g0s
            corr += coef_ref[4, j : j + 1, :] * g1 + coef_ref[5, j : j + 1, :] * g1s
        out_ref[rows, 0, 2 * LANES : 3 * LANES] = grad0
        out_ref[rows, 0, 3 * LANES : 4 * LANES] = grad1
        corr_ref[rows] = corr
    corr_ref[BLOCKS:] = zeros[:8]
    after = swap(corr_ref[1 : BLOCKS + 1])
    out_ref[:, 0, 4 * LANES :] = corr_ref[:BLOCKS] + jnp.where(real_lane, after, -after)


def inverse_kernel(
    in_ref, query_ref, key_ref, values_ref, cot_ref, gain_ref, last_ref, twiddle_ref, high_ref, low_ref,
    out_ref, grad_query_ref, grad_key_ref, grad_values_ref, grad_filter_ref, rows_ref,
):
    f32, bf16 = jnp.float32, jnp.bfloat16
    spectra = []
    for s in range(SIGNALS):
        cols = slice(LANES * s, LANES * (s + 1))
        spectra.append(jnp.concatenate([in_ref[:ROWS, 0, cols], in_ref[ROWS:, 0, cols]], 1))
    spread = dot3(jnp.concatenate(spectra, 0), high_ref[...], low_ref[...])
    tw_re, tw_im = twiddle_ref[0], twiddle_ref[1]
    real, imag = [], []
    for s in range(SIGNALS):
        re, im = spread[ROWS * s : ROWS * (s + 1), :LANES], spread[ROWS * s : ROWS * (s + 1), LANES:]
        real.append(re * tw_re + im * tw_im)
        imag.append(im * tw_re - re * tw_im)
    turned = jnp.concatenate([jnp.concatenate(real, 1), jnp.concatenate(imag, 1)], 0)
    high, low = split(turned)
    result = dot(last_ref[...], jnp.concatenate([high, high, low], 0))
    for s in range(4):
        rows_ref[s] = result[:, LANES * s : LANES * (s + 1)]
    grad_filter = result[:, 4 * LANES :]
    for copy in range(grad_filter_ref.shape[0]):
        grad_filter_ref[copy] = grad_filter
    gain = gain_ref[...]
    for j in range(ROWS):
        cols = slice(LANES * j, LANES * (j + 1))
        query, cot = query_ref[:, cols].astype(f32), cot_ref[:, cols].astype(f32)
        key, value = key_ref[:, cols].astype(f32), values_ref[:, cols].astype(f32)
        summed = rows_ref[0:2, j, :] + gain * (key * value)
        out_ref[:, cols] = (query * summed).astype(bf16)
        grad_query_ref[:, cols] = (cot * summed).astype(bf16)
        grad_mixed = rows_ref[2:4, j, :] + gain * (cot * query)
        grad_key_ref[:, cols] = (grad_mixed * value).astype(bf16)
        grad_values_ref[:, cols] = (grad_mixed * key).astype(bf16)


def per_device(gate_q, gate_k, values, filter_taps, skip_gain, cotangent):
    f32 = jnp.float32
    first, last, twiddle, second, second_back = jax.tree.map(jnp.asarray, make_tables())
    groups = lax.axis_size("chan")
    traffic = jax.ShapeDtypeStruct((BLOCKS, 1, WIDTH), f32)
    sent = pl.pallas_call(
        forward_kernel,
        out_shape=traffic,
        scratch_shapes=[pltpu.VMEM((4, ROWS, LANES), f32)],
        name="forward_transform",
    )(gate_k, values, cotangent, gate_q, filter_taps.reshape(ROWS, LANES), first, twiddle, *second)
    blocks = lax.all_to_all(sent, "ctx", 0, 0, tiled=True)
    sent = pl.pallas_call(
        blocks_kernel,
        out_shape=traffic,
        scratch_shapes=[
            pltpu.VMEM((4, 2 * BLOCKS, LANES), f32),
            pltpu.VMEM((4, 2 * BLOCKS, LANES), f32),
            pltpu.VMEM((6, BLOCKS, LANES), f32),
            pltpu.VMEM((BLOCKS + 8, LANES), f32),
        ],
        name="block_convolutions",
    )(blocks)
    spectra = lax.all_to_all(sent, "ctx", 0, 0, tiled=True)
    like = jax.ShapeDtypeStruct(gate_q.shape, jnp.bfloat16)
    *gated, partial_filter = pl.pallas_call(
        inverse_kernel,
        out_shape=(like, like, like, like, jax.ShapeDtypeStruct((groups, ROWS, LANES), f32)),
        scratch_shapes=[pltpu.VMEM((4, ROWS, LANES), f32)],
        name="inverse_transform",
    )(spectra, gate_q, gate_k, values, cotangent, skip_gain[:, None], last, twiddle, *second_back)
    grad_filter = jnp.sum(lax.all_to_all(partial_filter, "chan", 0, 0, tiled=True), axis=0)
    return (*gated, grad_filter.reshape(BLOCK))


def solution(mesh):
    return jax.shard_map(
        per_device,
        mesh=mesh,
        in_specs=(
            P("chan", "ctx"),
            P("chan", "ctx"),
            P("chan", "ctx"),
            P("ctx"),
            P("chan"),
            P("chan", "ctx"),
        ),
        out_specs=(
            P("chan", "ctx"),
            P("chan", "ctx"),
            P("chan", "ctx"),
            P("chan", "ctx"),
            P("ctx"),
        ),
        check_vma=False,
    )
```

profile of v0, /device:TPU:1, one launch (start us, length us, event | category | flops | bytes accessed | tf_op | source)
XLA Modules:
  0.0 74.5 jit_solution(1979299959126037726)
XLA Ops:
  0.6 2.2 %forward_transform.1 = f32[64,1,640]{2,1,0:T(1,128)} custom-call(bf16[2,4096]{1,0:T(2,128)(2,1)} %key_ref.3, bf16[2,4096]{1,0:T(2,128)(2,1)} %values_ref.3, bf16[2,4096]{1,0:T(2,128)(2,1)} %cot_ref.3, bf16[2,4096]{1,0:T(2,128)(2,1)} %query_ref.3, f32[32,128]{1,0:T(8,128)} %bitcast.3, bf16[64,96]{1,0:T(8,128)(2,1)} %constant.16.clone.first_ref, ...), custom_call_target="tpu_custom_call" | custom-call | tf_op jit(solution)/shard_map/forward_transform/pallas_call | solution.py:188
  2.9 33.5 %all_to_all.15.in_ref = f32[64,1,640]{2,1,0:T(1,128)} all-to-all(f32[64,1,640]{2,1,0:T(1,128)} %forward_transform.1), channel_id=1, replica_groups=mesh['ctx'=64,'chan'=8] {'ctx'}, dimensions={0} | all-to-all | bytes 327680 | tf_op jit(solution)/shard_map/all_to_all | solution.py:194
  36.3 3.5 %block_convolutions.1 = f32[64,1,640]{2,1,0:T(1,128)} custom-call(f32[64,1,640]{2,1,0:T(1,128)} %all_to_all.15.in_ref), custom_call_target="tpu_custom_call" | custom-call | tf_op jit(solution)/shard_map/block_convolutions/pallas_call | solution.py:195
  39.8 5.9 %all-to-all-start.1 = ((f32[64,1,640]{2,1,0:T(1,128)}), f32[64,1,640]{2,1,0:T(1,128)S(1)}, u32[]{:S(2)}, u32[]{:S(2)}) async-start(f32[64,1,640]{2,1,0:T(1,128)} %block_convolutions.1), calls=%async_computation.1 | async-start | bytes 327680 | tf_op jit(solution)/shard_map/all_to_all | solution.py:206
  45.8 0.0 copy-start.1
  45.8 0.6 copy-done.1
  46.4 0.6 copy.18.gain_ref
  47.1 12.4 %all-to-all-done.1.in_ref = f32[64,1,640]{2,1,0:T(1,128)S(1)} async-done(((f32[64,1,640]{2,1,0:T(1,128)}), f32[64,1,640]{2,1,0:T(1,128)S(1)}, u32[]{:S(2)}, u32[]{:S(2)}) %all-to-all-start.1) | async-done | bytes 163872 | tf_op jit(solution)/shard_map/all_to_all | solution.py:206
  59.5 0.0 copy-start
  59.5 0.7 copy-done
  60.1 2.3 %inverse_transform.1 = (bf16[2,4096]{1,0:T(2,128)(2,1)}, bf16[2,4096]{1,0:T(2,128)(2,1)}, bf16[2,4096]{1,0:T(2,128)(2,1)}, bf16[2,4096]{1,0:T(2,128)(2,1)}, f32[8,32,128]{2,1,0:T(8,128)}) custom-call(f32[64,1,640]{2,1,0:T(1,128)} %copy-done, bf16[2,4096]{1,0:T(2,128)(2,1)} %query_ref.3, bf16[2,4096]{1,0:T(2,128)(2,1)} %key_ref.3, ...), custom_call_target="tpu_custom_call" | custom-call | tf_op jit(solution)/shard_map/inverse_transform/pallas_call | solution.py:208
  62.5 11.5 %all_to_all.16 = f32[8,32,128]{2,1,0:T(8,128)S(1)} all-to-all(f32[8,32,128]{2,1,0:T(8,128)} %get-tuple-element.14), channel_id=1, replica_groups=mesh['ctx'=64,'chan'=8] {'chan'}, dimensions={0} | all-to-all | bytes 262144 | tf_op jit(solution)/shard_map/all_to_all | solution.py:214
  73.9 0.6 reduce_sum.9
Async XLA Ops:
  39.8 19.6 %all-to-all-start.1 = ((f32[64,1,640]{2,1,0:T(1,128)}), f32[64,1,640]{2,1,0:T(1,128)S(1)}, u32[]{:S(2)}, u32[]{:S(2)}) async-start(f32[64,1,640]{2,1,0:T(1,128)} %block_convolutions.1), calls=%async_computation.1 | async-start | bytes 327680 | tf_op jit(solution)/shard_map/all_to_all | solution.py:206
  45.8 0.7 copy-start.1
  59.5 0.7 copy-start
where the time goes:
time: 74.9 us; the launch traced here: 74.5 us
  blocking collectives  44.9 us (60%)
  waiting for transfers between devices  12.4 us (17%)
  Pallas kernels  8.06 us (11%)
  starting transfers between devices  5.93 us (8%)
  local copies, waits for them, and re-layouts  1.96 us (3%)
    all_to_all x1, blocking collectives, per_device(): blocks = lax.all_to_all(sent, 'ctx', 0, 0, tiled=True)  33.5 us
    all_to_all x1, waiting for transfers between devices, per_device(): spectra = lax.all_to_all(sent, 'ctx', 0, 0, tiled=True)  12.4 us
    all_to_all x1, blocking collectives, per_device(): lax.all_to_all(partial_filter, 'chan', 0, 0, tiled=True)  11.5 us
    all_to_all x1, starting transfers between devices, per_device(): spectra = lax.all_to_all(sent, 'ctx', 0, 0, tiled=True)  5.93 us
    pallas_call x1, Pallas kernels, per_device(): pl.pallas_call(blocks_kernel, out_shape=traffic, scratch_shapes=[pltpu.VM...  3.51 us
    pallas_call x1, Pallas kernels, per_device(): pl.pallas_call(inverse_kernel, out_shape=(like, like, like, like, jax.Sha...  2.33 us
    pallas_call x1, Pallas kernels, per_device(): pl.pallas_call(forward_kernel, out_shape=traffic, scratch_shapes=[pltpu.V...  2.22 us
  transfers between devices with their start and end apart: 1, of which 1 were waited for; matrix products, arithmetic and copies ran while one was open for 1% of the time, Pallas kernels for 0%

commit v1 on v0

--- a/solution.py
+++ b/solution.py
@@ -14,6 +14,9 @@
 HALF = 64
 SIGNALS = 5
 WIDTH = SIGNALS * LANES
+FAR = 52
+CTX_ORDER = [[FAR if p == 0 else 0 if p == FAR else p for p in range(BLOCKS)]]
+CHAN_ORDER = [[4, 5, 2, 3, 6, 7, 0, 1]]
 
 
 def split(value):
@@ -88,7 +91,21 @@
     zeros = jnp.zeros((BLOCKS, LANES), jnp.float32)
 
     def signal(s):
-        return in_ref[:, 0, LANES * s : LANES * (s + 1)]
+        cols = slice(LANES * s, LANES * (s + 1))
+        return jnp.concatenate([in_ref[FAR : FAR + 1, 0, cols], in_ref[1:FAR, 0, cols], in_ref[0:1, 0, cols], in_ref[FAR + 1 :, 0, cols]], 0)
+
+    def put(first, value, s):
+        cols = slice(LANES * s, LANES * (s + 1))
+        if first == 0:
+            out_ref[FAR : FAR + 1, 0, cols] = value[0:1]
+            out_ref[1:8, 0, cols] = value[1:8]
+        elif first <= FAR < first + 8:
+            at = FAR - first
+            out_ref[first:FAR, 0, cols] = value[:at]
+            out_ref[0:1, 0, cols] = value[at : at + 1]
+            out_ref[FAR + 1 : first + 8, 0, cols] = value[at + 1 :]
+        else:
+            out_ref[first : first + 8, 0, cols] = value
 
     def swap(value):
         return pltpu.roll(value, HALF, 1)
@@ -123,8 +140,8 @@
             fa, fb = coef_ref[0, j : j + 1, :], coef_ref[1, j : j + 1, :]
             conv0 += fa * past_ref[0, window, :] + fb * past_ref[1, window, :]
             conv1 += fa * past_ref[2, window, :] + fb * past_ref[3, window, :]
-        out_ref[rows, 0, 0:LANES] = conv0
-        out_ref[rows, 0, LANES : 2 * LANES] = conv1
+        put(8 * r, conv0, 0)
+        put(8 * r, conv1, 1)
         grad0 = grad1 = corr = jnp.zeros((8, LANES), jnp.float32)
         for j in range(BLOCKS - 8 * r):
             window = slice(8 * r + j, 8 * r + j + 8)
@@ -135,12 +152,14 @@
             grad1 += fa * g1 - fb * g1s
             corr += coef_ref[2, j : j + 1, :] * g0 + coef_ref[3, j : j + 1, :] * g0s
             corr += coef_ref[4, j : j + 1, :] * g1 + coef_ref[5, j : j + 1, :] * g1s
-        out_ref[rows, 0, 2 * LANES : 3 * LANES] = grad0
-        out_ref[rows, 0, 3 * LANES : 4 * LANES] = grad1
+        put(8 * r, grad0, 2)
+        put(8 * r, grad1, 3)
         corr_ref[rows] = corr
     corr_ref[BLOCKS:] = zeros[:8]
     after = swap(corr_ref[1 : BLOCKS + 1])
-    out_ref[:, 0, 4 * LANES :] = corr_ref[:BLOCKS] + jnp.where(real_lane, after, -after)
+    taps_grad = corr_ref[:BLOCKS] + jnp.where(real_lane, after, -after)
+    for r in range(BLOCKS // 8):
+        put(8 * r, taps_grad[8 * r : 8 * r + 8], 4)
 
 
 def inverse_kernel(
@@ -167,7 +186,8 @@
     grad_filter = result[:, 4 * LANES :]
     for copy in range(grad_filter_ref.shape[0]):
         grad_filter_ref[copy] = grad_filter
-    gain = gain_ref[...]
+    first_channel = lax.broadcasted_iota(jnp.int32, (2, LANES), 0) == 0
+    gain = jnp.where(first_channel, gain_ref[0], gain_ref[1])
     for j in range(ROWS):
         cols = slice(LANES * j, LANES * (j + 1))
         query, cot = query_ref[:, cols].astype(f32), cot_ref[:, cols].astype(f32)
@@ -191,7 +211,7 @@
         scratch_shapes=[pltpu.VMEM((4, ROWS, LANES), f32)],
         name="forward_transform",
     )(gate_k, values, cotangent, gate_q, filter_taps.reshape(ROWS, LANES), first, twiddle, *second)
-    blocks = lax.all_to_all(sent, "ctx", 0, 0, tiled=True)
+    blocks = lax.all_to_all(sent, "ctx", 0, 0, tiled=True, axis_index_groups=CTX_ORDER)
     sent = pl.pallas_call(
         blocks_kernel,
         out_shape=traffic,
@@ -203,15 +223,17 @@
         ],
         name="block_convolutions",
     )(blocks)
-    spectra = lax.all_to_all(sent, "ctx", 0, 0, tiled=True)
+    spectra = lax.all_to_all(sent, "ctx", 0, 0, tiled=True, axis_index_groups=CTX_ORDER)
+    vmem = pl.BlockSpec(memory_space=pltpu.VMEM)
     like = jax.ShapeDtypeStruct(gate_q.shape, jnp.bfloat16)
     *gated, partial_filter = pl.pallas_call(
         inverse_kernel,
         out_shape=(like, like, like, like, jax.ShapeDtypeStruct((groups, ROWS, LANES), f32)),
+        in_specs=[vmem] * 5 + [pl.BlockSpec(memory_space=pltpu.SMEM)] + [vmem] * 4,
         scratch_shapes=[pltpu.VMEM((4, ROWS, LANES), f32)],
         name="inverse_transform",
-    )(spectra, gate_q, gate_k, values, cotangent, skip_gain[:, None], last, twiddle, *second_back)
-    grad_filter = jnp.sum(lax.all_to_all(partial_filter, "chan", 0, 0, tiled=True), axis=0)
+    )(spectra, gate_q, gate_k, values, cotangent, skip_gain, last, twiddle, *second_back)
+    grad_filter = jnp.sum(lax.all_to_all(partial_filter, "chan", 0, 0, tiled=True, axis_index_groups=CHAN_ORDER), axis=0)
     return (*gated, grad_filter.reshape(BLOCK))
 
 

time: 74.9 us -> 67.6 us (0.903)
  blocking collectives: 44.9 us -> 57.9 us
  waiting for transfers between devices: 12.4 us -> 0 us
  starting transfers between devices: 5.93 us -> 0 us
  local copies, waits for them, and re-layouts: 1.96 us -> 0 us
    all_to_all x2 -> x3, blocking collectives: 44.9 us -> 57.9 us  [the longest x2 45.5 us: per_device(): lax.all_to_all(sent, 'ctx', 0, 0, tiled=True, axis_index_groups=CTX_ORDER)]
    all_to_all x1 -> x0, waiting for transfers between devices: 12.4 us -> none  [per_device(): spectra = lax.all_to_all(sent, 'ctx', 0, 0, tiled=True)]
    all_to_all x1 -> x0, starting transfers between devices: 5.93 us -> none  [per_device(): spectra = lax.all_to_all(sent, 'ctx', 0, 0, tiled=True)]
    unnamed x4 -> x0, local copies, waits for them, and re-layouts: 1.31 us -> none
  transfers between devices with their start and end apart: 1 -> 0, of which waited for: 1 -> 0; matrix products, arithmetic and copies ran while one was open for 1% -> 0% of each run, Pallas kernels for 0% -> 0%
where the time goes in v1:
time: 67.6 us; the launch traced here: 67.2 us
  blocking collectives  57.9 us (86%)
  Pallas kernels  8.01 us (12%)
    all_to_all x2, blocking collectives, per_device(): lax.all_to_all(sent, 'ctx', 0, 0, tiled=True, axis_index_groups=CTX_ORDER)  45.5 us
    all_to_all x1, blocking collectives, per_device(): lax.all_to_all(partial_filter, 'chan', 0, 0, tiled=True, axis_index_group...  12.3 us
    pallas_call x1, Pallas kernels, per_device(): pl.pallas_call(blocks_kernel, out_shape=traffic, scratch_shapes=[pltpu.VM...  3.5 us
    pallas_call x1, Pallas kernels, per_device(): pl.pallas_call(inverse_kernel, out_shape=(like, like, like, like, jax.Sha...  2.31 us
    pallas_call x1, Pallas kernels, per_device(): pl.pallas_call(forward_kernel, out_shape=traffic, scratch_shapes=[pltpu.V...  2.21 us

profile of v1, /device:TPU:1, one launch (start us, length us, event | category | flops | bytes accessed | tf_op | source)
XLA Modules:
  0.0 67.2 jit_solution(9127003775878855542)
XLA Ops:
  0.6 2.2 %forward_transform.1 = f32[64,1,640]{2,1,0:T(1,128)} custom-call(bf16[2,4096]{1,0:T(2,128)(2,1)} %key_ref.3, bf16[2,4096]{1,0:T(2,128)(2,1)} %values_ref.3, bf16[2,4096]{1,0:T(2,128)(2,1)} %cot_ref.3, bf16[2,4096]{1,0:T(2,128)(2,1)} %query_ref.3, f32[32,128]{1,0:T(8,128)} %bitcast.2, bf16[64,96]{1,0:T(8,128)(2,1)} %constant.16.clone.first_ref, ...), custom_call_target="tpu_custom_call" | custom-call | tf_op jit(solution)/shard_map/forward_transform/pallas_call | solution.py:208
  2.8 27.2 %all_to_all.15.in_ref = f32[64,1,640]{2,1,0:T(1,128)} all-to-all(f32[64,1,640]{2,1,0:T(1,128)} %forward_transform.1), channel_id=1, replica_groups={{416,8,16,24,32,40,48,56,64,72,80,88,96,104,112,120,128,136,144,152,160..., dimensions={0} | all-to-all | bytes 327680 | tf_op jit(solution)/shard_map/all_to_all | solution.py:214
  30.0 3.5 %block_convolutions.1 = f32[64,1,640]{2,1,0:T(1,128)} custom-call(f32[64,1,640]{2,1,0:T(1,128)} %all_to_all.15.in_ref), custom_call_target="tpu_custom_call" | custom-call | tf_op jit(solution)/shard_map/block_convolutions/pallas_call | solution.py:215
  33.5 18.3 %all_to_all.16.in_ref = f32[64,1,640]{2,1,0:T(1,128)} all-to-all(f32[64,1,640]{2,1,0:T(1,128)} %block_convolutions.1), channel_id=1, replica_groups={{416,8,16,24,32,40,48,56,64,72,80,88,96,104,112,120,128,136,144,152,160..., dimensions={0} | all-to-all | bytes 327680 | tf_op jit(solution)/shard_map/all_to_all | solution.py:226
  51.9 2.3 %inverse_transform.1 = (bf16[2,4096]{1,0:T(2,128)(2,1)}, bf16[2,4096]{1,0:T(2,128)(2,1)}, bf16[2,4096]{1,0:T(2,128)(2,1)}, bf16[2,4096]{1,0:T(2,128)(2,1)}, f32[8,32,128]{2,1,0:T(8,128)}) custom-call(f32[64,1,640]{2,1,0:T(1,128)} %all_to_all.16.in_ref, bf16[2,4096]{1,0:T(2,128)(2,1)} %query_ref.3, bf16[2,4096]{1,0:T(2,128)(2,1)} %key_ref.3, ...), custom_call_target="tpu_custom_call" | custom-call | tf_op jit(solution)/shard_map/inverse_transform/pallas_call | solution.py:229
  54.2 12.3 %all_to_all.17 = f32[8,32,128]{2,1,0:T(8,128)S(1)} all-to-all(f32[8,32,128]{2,1,0:T(8,128)} %get-tuple-element.14), channel_id=1, replica_groups={{4,5,2,3,6,7,0,1},{12,13,10,11,14,15,8,9},{20,21,18,19,22,23,16,17},{28..., dimensions={0} | all-to-all | bytes 262144 | tf_op jit(solution)/shard_map/all_to_all | solution.py:236
  66.5 0.6 reduce_sum.9

commit v2 on v1

--- a/solution.py
+++ b/solution.py
@@ -14,6 +14,7 @@
 HALF = 64
 SIGNALS = 5
 WIDTH = SIGNALS * LANES
+SMALL = pltpu.CompilerParams(vmem_limit_bytes=8 << 20)
 FAR = 52
 CTX_ORDER = [[FAR if p == 0 else 0 if p == FAR else p for p in range(BLOCKS)]]
 CHAN_ORDER = [[4, 5, 2, 3, 6, 7, 0, 1]]
@@ -209,6 +210,7 @@
         forward_kernel,
         out_shape=traffic,
         scratch_shapes=[pltpu.VMEM((4, ROWS, LANES), f32)],
+        compiler_params=SMALL,
         name="forward_transform",
     )(gate_k, values, cotangent, gate_q, filter_taps.reshape(ROWS, LANES), first, twiddle, *second)
     blocks = lax.all_to_all(sent, "ctx", 0, 0, tiled=True, axis_index_groups=CTX_ORDER)
@@ -221,6 +223,7 @@
             pltpu.VMEM((6, BLOCKS, LANES), f32),
             pltpu.VMEM((BLOCKS + 8, LANES), f32),
         ],
+        compiler_params=SMALL,
         name="block_convolutions",
     )(blocks)
     spectra = lax.all_to_all(sent, "ctx", 0, 0, tiled=True, axis_index_groups=CTX_ORDER)
@@ -231,6 +234,7 @@
         out_shape=(like, like, like, like, jax.ShapeDtypeStruct((groups, ROWS, LANES), f32)),
         in_specs=[vmem] * 5 + [pl.BlockSpec(memory_space=pltpu.SMEM)] + [vmem] * 4,
         scratch_shapes=[pltpu.VMEM((4, ROWS, LANES), f32)],
+        compiler_params=SMALL,
         name="inverse_transform",
     )(spectra, gate_q, gate_k, values, cotangent, skip_gain, last, twiddle, *second_back)
     grad_filter = jnp.sum(lax.all_to_all(partial_filter, "chan", 0, 0, tiled=True, axis_index_groups=CHAN_ORDER), axis=0)

time: 67.6 us -> 69.2 us (1.024); the launches traced: 67.2 us -> 68 us
  local copies, waits for them, and re-layouts: 0 us -> 6.91 us
  Pallas kernels: 8.01 us -> 4.05 us
  blocking collectives: 57.9 us -> 55.7 us
    unnamed x0 -> x36, local copies, waits for them, and re-layouts: none -> 6.91 us
    all_to_all x1, blocking collectives: 12.3 us -> 9.33 us  [per_device(): lax.all_to_all(partial_filter, 'chan', 0, 0, tiled=True, axis_index_group...]
    pallas_call x1, Pallas kernels: 2.21 us -> 0.45 us  [per_device(): pl.pallas_call(forward_kernel, out_shape=traffic, scratch_shapes=[pltpu.V...]
    pallas_call x1, Pallas kernels: 3.5 us -> 1.94 us  [per_device(): pl.pallas_call(blocks_kernel, out_shape=traffic, scratch_shapes=[pltpu.VM...]
    all_to_all x2, blocking collectives: 45.5 us -> 46.3 us  [per_device(): lax.all_to_all(sent, 'ctx', 0, 0, tiled=True, axis_index_groups=CTX_ORDER)]
where the time goes in v2:
time: 69.2 us; the launch traced here: 68 us
  blocking collectives  55.7 us (80%)
  local copies, waits for them, and re-layouts  6.91 us (10%)
  Pallas kernels  4.05 us (6%)
  between operations  0.76 us (1%)
    all_to_all x2, blocking collectives, per_device(): lax.all_to_all(sent, 'ctx', 0, 0, tiled=True, axis_index_groups=CTX_ORDER)  46.3 us
    all_to_all x1, blocking collectives, per_device(): lax.all_to_all(partial_filter, 'chan', 0, 0, tiled=True, axis_index_group...  9.33 us
    unnamed x36, local copies, waits for them, and re-layouts  6.91 us
    pallas_call x1, Pallas kernels, per_device(): pl.pallas_call(blocks_kernel, out_shape=traffic, scratch_shapes=[pltpu.VM...  1.94 us
    pallas_call x1, Pallas kernels, per_device(): pl.pallas_call(inverse_kernel, out_shape=(like, like, like, like, jax.Sha...  1.66 us

profile of v2, /device:TPU:1, one launch (start us, length us, event | category | flops | bytes accessed | tf_op | source)
XLA Modules:
  0.0 68.0 jit_solution(4509982906686161426)
XLA Ops:
  0.6 0.0 copy-start.2
  0.6 0.9 %copy-done.2 = bf16[256,256]{1,0:T(8,128)(2,1)S(1)} copy-done((bf16[256,256]{1,0:T(8,128)(2,1)S(1)}, bf16[256,256]{1,0:T(8,128)(2,1)}, u32[]{:S(2)}) %copy-start.2) | copy-done | bytes 131096
  1.5 0.0 copy-start.3
  1.5 0.9 %copy-done.3 = bf16[256,256]{1,0:T(8,128)(2,1)S(1)} copy-done((bf16[256,256]{1,0:T(8,128)(2,1)S(1)}, bf16[256,256]{1,0:T(8,128)(2,1)}, u32[]{:S(2)}) %copy-start.3) | copy-done | bytes 131096
  2.4 0.0 copy-start.4
  2.4 0.8 %copy-done.4 = f32[2,32,128]{2,1,0:T(8,128)S(1)} copy-done((f32[2,32,128]{2,1,0:T(8,128)S(1)}, f32[2,32,128]{2,1,0:T(8,128)}, u32[]{:S(2)}) %copy-start.4) | copy-done | bytes 32792
  3.2 0.0 copy-start.6
  3.2 0.7 %copy-done.6 = bf16[2,4096]{1,0:T(2,128)(2,1)S(1)} copy-done((bf16[2,4096]{1,0:T(2,128)(2,1)S(1)}, bf16[2,4096]{1,0:T(2,128)(2,1)}, u32[]{:S(2)}) %copy-start.6) | copy-done | bytes 16408
  3.9 0.0 copy-start.8
  3.9 0.7 %copy-done.8 = bf16[2,4096]{1,0:T(2,128)(2,1)S(1)} copy-done((bf16[2,4096]{1,0:T(2,128)(2,1)S(1)}, bf16[2,4096]{1,0:T(2,128)(2,1)}, u32[]{:S(2)}) %copy-start.8) | copy-done | bytes 16408
  4.6 0.0 copy-start.10
  4.6 0.7 %copy-done.10 = bf16[2,4096]{1,0:T(2,128)(2,1)S(1)} copy-done((bf16[2,4096]{1,0:T(2,128)(2,1)S(1)}, bf16[2,4096]{1,0:T(2,128)(2,1)}, u32[]{:S(2)}) %copy-start.10) | copy-done | bytes 16408
  5.4 0.0 copy-start.12
  5.4 0.7 %copy-done.12 = bf16[2,4096]{1,0:T(2,128)(2,1)S(1)} copy-done((bf16[2,4096]{1,0:T(2,128)(2,1)S(1)}, bf16[2,4096]{1,0:T(2,128)(2,1)}, u32[]{:S(2)}) %copy-start.12) | copy-done | bytes 16408
  6.1 0.0 copy-start.14
  6.1 0.7 %copy-done.14 = f32[4096]{0:T(1024)S(1)} copy-done((f32[4096]{0:T(1024)S(1)}, f32[4096]{0:T(1024)}, u32[]{:S(2)}) %copy-start.14) | copy-done | bytes 16408
  6.8 0.0 copy-start.16
  6.8 0.7 %copy-done.16 = bf16[64,96]{1,0:T(8,128)(2,1)S(1)} copy-done((bf16[64,96]{1,0:T(8,128)(2,1)S(1)}, bf16[64,96]{1,0:T(8,128)(2,1)}, u32[]{:S(2)}) %copy-start.16) | copy-done | bytes 12312
  7.5 0.5 forward_transform.1
  8.0 26.9 %all_to_all.15.in_ref = f32[64,1,640]{2,1,0:T(1,128)S(1)} all-to-all(f32[64,1,640]{2,1,0:T(1,128)S(1)} %forward_transform.1), channel_id=1, replica_groups={{416,8,16,24,32,40,48,56,64,72,80,88,96,104,112,120,128,136,144,152,160..., dimensions={0} | all-to-all | bytes 327680 | tf_op jit(solution)/shard_map/all_to_all | solution.py:216
  34.9 0.0 copy-start.11
  34.9 0.0 copy-start.13
  34.9 0.0 copy-start.15
  34.9 0.0 copy-start.17
  34.9 1.9 %block_convolutions.1 = f32[64,1,640]{2,1,0:T(1,128)S(1)} custom-call(f32[64,1,640]{2,1,0:T(1,128)S(1)} %all_to_all.15.in_ref), custom_call_target="tpu_custom_call" | custom-call | tf_op jit(solution)/shard_map/block_convolutions/pallas_call | solution.py:217
  36.8 0.0 copy-start
  36.8 0.0 copy-start.1
  36.8 0.0 copy-start.5
  36.9 0.0 copy-start.7
  36.9 0.0 copy-start.9
  36.9 19.4 %all_to_all.16.in_ref = f32[64,1,640]{2,1,0:T(1,128)S(1)} all-to-all(f32[64,1,640]{2,1,0:T(1,128)S(1)} %block_convolutions.1), channel_id=1, replica_groups={{416,8,16,24,32,40,48,56,64,72,80,88,96,104,112,120,128,136,144,152,160..., dimensions={0} | all-to-all | bytes 327680 | tf_op jit(solution)/shard_map/all_to_all | solution.py:229
  56.3 0.0 copy-done.11
  56.3 0.0 copy-done.13
  56.3 0.0 copy-done.15
  56.3 0.0 copy-done.17
  56.3 0.0 copy-done
  56.3 0.0 copy-done.1
  56.4 0.0 copy-done.5
  56.4 0.0 copy-done.7
  56.4 0.0 copy-done.9
  56.4 1.7 %inverse_transform.1 = (bf16[2,4096]{1,0:T(2,128)(2,1)}, bf16[2,4096]{1,0:T(2,128)(2,1)}, bf16[2,4096]{1,0:T(2,128)(2,1)}, bf16[2,4096]{1,0:T(2,128)(2,1)}, f32[8,32,128]{2,1,0:T(8,128)S(1)}) custom-call(f32[64,1,640]{2,1,0:T(1,128)S(1)} %all_to_all.16.in_ref, bf16[2,4096]{1,0:T(2,128)(2,1)S(1)} %copy-done.13, bf16[2,4096]{1,0:T(2,128)(2,1)S(1)} %copy-done.7, ...), custom_call_target="tpu_custom_call" | custom-call | tf_op jit(solution)/shard_map/inverse_transform/pallas_call | solution.py:232
  58.0 9.3 %all_to_all.17 = f32[8,32,128]{2,1,0:T(8,128)S(1)} all-to-all(f32[8,32,128]{2,1,0:T(8,128)S(1)} %get-tuple-element.14), channel_id=1, replica_groups={{4,5,2,3,6,7,0,1},{12,13,10,11,14,15,8,9},{20,21,18,19,22,23,16,17},{28..., dimensions={0} | all-to-all | bytes 262144 | tf_op jit(solution)/shard_map/all_to_all | solution.py:240
  67.4 0.6 reduce_sum.9
Async XLA Ops:
  0.6 0.9 %copy-start.2 = (bf16[256,256]{1,0:T(8,128)(2,1)S(1)}, bf16[256,256]{1,0:T(8,128)(2,1)}, u32[]{:S(2)}) copy-start(bf16[256,256]{1,0:T(8,128)(2,1)} %constant.20.clone.low_ref) | copy-start | bytes 393220
  1.5 0.9 %copy-start.3 = (bf16[256,256]{1,0:T(8,128)(2,1)S(1)}, bf16[256,256]{1,0:T(8,128)(2,1)}, u32[]{:S(2)}) copy-start(bf16[256,256]{1,0:T(8,128)(2,1)} %constant.19.clone.high_ref) | copy-start | bytes 393220
  2.4 0.8 %copy-start.4 = (f32[2,32,128]{2,1,0:T(8,128)S(1)}, f32[2,32,128]{2,1,0:T(8,128)}, u32[]{:S(2)}) copy-start(f32[2,32,128]{2,1,0:T(8,128)} %constant.18.clone.twiddle_ref) | copy-start | bytes 98308
  3.2 0.7 %copy-start.6 = (bf16[2,4096]{1,0:T(2,128)(2,1)S(1)}, bf16[2,4096]{1,0:T(2,128)(2,1)}, u32[]{:S(2)}) copy-start(bf16[2,4096]{1,0:T(2,128)(2,1)} %key_ref.3) | copy-start | bytes 49156
  3.9 0.7 %copy-start.8 = (bf16[2,4096]{1,0:T(2,128)(2,1)S(1)}, bf16[2,4096]{1,0:T(2,128)(2,1)}, u32[]{:S(2)}) copy-start(bf16[2,4096]{1,0:T(2,128)(2,1)} %values_ref.3) | copy-start | bytes 49156
  4.6 0.7 %copy-start.10 = (bf16[2,4096]{1,0:T(2,128)(2,1)S(1)}, bf16[2,4096]{1,0:T(2,128)(2,1)}, u32[]{:S(2)}) copy-start(bf16[2,4096]{1,0:T(2,128)(2,1)} %cot_ref.3) | copy-start | bytes 49156
  5.4 0.7 %copy-start.12 = (bf16[2,4096]{1,0:T(2,128)(2,1)S(1)}, bf16[2,4096]{1,0:T(2,128)(2,1)}, u32[]{:S(2)}) copy-start(bf16[2,4096]{1,0:T(2,128)(2,1)} %query_ref.3) | copy-start | bytes 49156
  6.1 0.7 %copy-start.14 = (f32[4096]{0:T(1024)S(1)}, f32[4096]{0:T(1024)}, u32[]{:S(2)}) copy-start(f32[4096]{0:T(1024)} %param.16) | copy-start | bytes 49156
  6.8 0.7 %copy-start.16 = (bf16[64,96]{1,0:T(8,128)(2,1)S(1)}, bf16[64,96]{1,0:T(8,128)(2,1)}, u32[]{:S(2)}) copy-start(bf16[64,96]{1,0:T(8,128)(2,1)} %constant.16.clone.first_ref) | copy-start | bytes 36868
  34.9 21.4 %copy-start.11 = (bf16[2,4096]{1,0:T(2,128)(2,1)S(1)}, bf16[2,4096]{1,0:T(2,128)(2,1)}, u32[]{:S(2)}) copy-start(bf16[2,4096]{1,0:T(2,128)(2,1)} %cot_ref.3) | copy-start | bytes 49156
  34.9 21.4 %copy-start.13 = (bf16[2,4096]{1,0:T(2,128)(2,1)S(1)}, bf16[2,4096]{1,0:T(2,128)(2,1)}, u32[]{:S(2)}) copy-start(bf16[2,4096]{1,0:T(2,128)(2,1)} %query_ref.3) | copy-start | bytes 49156
  34.9 21.4 %copy-start.15 = (bf16[32,192]{1,0:T(8,128)(2,1)S(1)}, bf16[32,192]{1,0:T(8,128)(2,1)}, u32[]{:S(2)}) copy-start(bf16[32,192]{1,0:T(8,128)(2,1)} %constant.17.clone.last_ref) | copy-start | bytes 36868
  34.9 21.5 %copy-start.17 = (f32[2]{0:T(128)S(1)}, f32[2]{0:T(128)}, u32[]{:S(2)}) copy-start(f32[2]{0:T(128)} %gain_ref.1) | copy-start | bytes 28
  36.8 19.5 %copy-start = (bf16[256,256]{1,0:T(8,128)(2,1)S(1)}, bf16[256,256]{1,0:T(8,128)(2,1)}, u32[]{:S(2)}) copy-start(bf16[256,256]{1,0:T(8,128)(2,1)} %constant.22.clone.low_ref) | copy-start | bytes 393220
  36.8 19.5 %copy-start.1 = (bf16[256,256]{1,0:T(8,128)(2,1)S(1)}, bf16[256,256]{1,0:T(8,128)(2,1)}, u32[]{:S(2)}) copy-start(bf16[256,256]{1,0:T(8,128)(2,1)} %constant.21.clone.high_ref) | copy-start | bytes 393220
  36.8 19.5 %copy-start.5 = (f32[2,32,128]{2,1,0:T(8,128)S(1)}, f32[2,32,128]{2,1,0:T(8,128)}, u32[]{:S(2)}) copy-start(f32[2,32,128]{2,1,0:T(8,128)} %constant.18.clone.twiddle_ref) | copy-start | bytes 98308
  36.9 19.5 %copy-start.7 = (bf16[2,4096]{1,0:T(2,128)(2,1)S(1)}, bf16[2,4096]{1,0:T(2,128)(2,1)}, u32[]{:S(2)}) copy-start(bf16[2,4096]{1,0:T(2,128)(2,1)} %key_ref.3) | copy-start | bytes 49156
  36.9 19.5 %copy-start.9 = (bf16[2,4096]{1,0:T(2,128)(2,1)S(1)}, bf16[2,4096]{1,0:T(2,128)(2,1)}, u32[]{:S(2)}) copy-start(bf16[2,4096]{1,0:T(2,128)(2,1)} %values_ref.3) | copy-start | bytes 49156

commit v3 on v2

--- a/solution.py
+++ b/solution.py
@@ -51,6 +51,25 @@
     return first_table, last_table, twiddle, split_table(second), split_table(second.T)
 
 
+def make_block_tables():
+    blocks = np.array(CTX_ORDER[0])
+    phases = np.arange(2 * BLOCKS)
+    wave = np.exp(-2j * np.pi * phases[:, None] * blocks[None, :] / (2 * BLOCKS))
+    step = np.exp(-2j * np.pi * phases / (2 * BLOCKS))
+    back = np.conj(wave.T) / (2 * BLOCKS)
+
+    def there(table):
+        high, low = split_table(np.concatenate([table.real, -table.imag], 0))
+        return np.concatenate([high, low, high], 1)
+
+    def here(table):
+        return split_table(np.concatenate([table.real, table.imag], 1))
+
+    filter_wave = wave * (1 + 1j * step)[:, None]
+    filter_back = back * (1 - 1j * np.conj(step))[None, :]
+    return there(wave), there(filter_wave), *here(back), *here(filter_back)
+
+
 def dot(left, right):
     return jnp.dot(left, right, preferred_element_type=jnp.float32)
 
@@ -60,9 +79,14 @@
     return dot(value_high, high) + (dot(value_high, low) + dot(value_low, high))
 
 
-def forward_kernel(
-    key_ref, values_ref, cot_ref, query_ref, taps_ref, first_ref, twiddle_ref, high_ref, low_ref, out_ref, rows_ref
-):
+def forward_kernel(*refs):
+    operands, (out_ref, *held, rows_ref, sems) = refs[:9], refs[9:]
+    copies = [pltpu.make_async_copy(src, dst, sems.at[n]) for n, (src, dst) in enumerate(zip(operands, held))]
+    for copy in copies:
+        copy.start()
+    for copy in copies:
+        copy.wait()
+    key_ref, values_ref, cot_ref, query_ref, taps_ref, first_ref, twiddle_ref, high_ref, low_ref = held
     f32 = jnp.float32
     mixed = key_ref[...].astype(f32) * values_ref[...].astype(f32)
     grad = cot_ref[...].astype(f32) * query_ref[...].astype(f32)
@@ -87,80 +111,47 @@
             ]
 
 
-def blocks_kernel(in_ref, out_ref, past_ref, next_ref, coef_ref, corr_ref):
-    real_lane = lax.broadcasted_iota(jnp.int32, (BLOCKS, LANES), 1) < HALF
-    zeros = jnp.zeros((BLOCKS, LANES), jnp.float32)
-
-    def signal(s):
-        cols = slice(LANES * s, LANES * (s + 1))
-        return jnp.concatenate([in_ref[FAR : FAR + 1, 0, cols], in_ref[1:FAR, 0, cols], in_ref[0:1, 0, cols], in_ref[FAR + 1 :, 0, cols]], 0)
-
-    def put(first, value, s):
-        cols = slice(LANES * s, LANES * (s + 1))
-        if first == 0:
-            out_ref[FAR : FAR + 1, 0, cols] = value[0:1]
-            out_ref[1:8, 0, cols] = value[1:8]
-        elif first <= FAR < first + 8:
-            at = FAR - first
-            out_ref[first:FAR, 0, cols] = value[:at]
-            out_ref[0:1, 0, cols] = value[at : at + 1]
-            out_ref[FAR + 1 : first + 8, 0, cols] = value[at + 1 :]
-        else:
-            out_ref[first : first + 8, 0, cols] = value
-
-    def swap(value):
-        return pltpu.roll(value, HALF, 1)
-
-    taps = signal(4)
-    corr_ref[0:8] = zeros[:8]
-    corr_ref[8:72] = taps
-    before = swap(corr_ref[7:71])
-    taps = taps + jnp.where(real_lane, -before, before)
-    swapped = swap(taps)
-    coef_ref[0] = jnp.where(real_lane, taps, swapped)
-    coef_ref[1] = jnp.where(real_lane, -swapped, taps)
-    for c in range(2):
-        mixed, grad = signal(c), signal(2 + c)
-        mixed_swap = swap(mixed)
-        past_ref[2 * c, 0:BLOCKS] = zeros
-        past_ref[2 * c, BLOCKS:] = mixed
-        past_ref[2 * c + 1, 0:BLOCKS] = zeros
-        past_ref[2 * c + 1, BLOCKS:] = mixed_swap
-        next_ref[2 * c, 0:BLOCKS] = grad
-        next_ref[2 * c, BLOCKS:] = zeros
-        next_ref[2 * c + 1, 0:BLOCKS] = swap(grad)
-        next_ref[2 * c + 1, BLOCKS:] = zeros
-        coef_ref[2 + 2 * c] = jnp.where(real_lane, mixed, mixed_swap)
-        coef_ref[3 + 2 * c] = jnp.where(real_lane, mixed_swap, -mixed)
-
-    for r in range(BLOCKS // 8):
-        rows = slice(8 * r, 8 * r + 8)
-        conv0 = conv1 = jnp.zeros((8, LANES), jnp.float32)
-        for j in range(8 * r + 8):
-            window = slice(BLOCKS + 8 * r - j, BLOCKS + 8 * r - j + 8)
-            fa, fb = coef_ref[0, j : j + 1, :], coef_ref[1, j : j + 1, :]
-            conv0 += fa * past_ref[0, window, :] + fb * past_ref[1, window, :]
-            conv1 += fa * past_ref[2, window, :] + fb * past_ref[3, window, :]
-        put(8 * r, conv0, 0)
-        put(8 * r, conv1, 1)
-        grad0 = grad1 = corr = jnp.zeros((8, LANES), jnp.float32)
-        for j in range(BLOCKS - 8 * r):
-            window = slice(8 * r + j, 8 * r + j + 8)
-            fa, fb = coef_ref[0, j : j + 1, :], coef_ref[1, j : j + 1, :]
-            g0, g0s = next_ref[0, window, :], next_ref[1, window, :]
-            g1, g1s = next_ref[2, window, :], next_ref[3, window, :]
-            grad0 += fa * g0 - fb * g0s
-            grad1 += fa * g1 - fb * g1s
-            corr += coef_ref[2, j : j + 1, :] * g0 + coef_ref[3, j : j + 1, :] * g0s
-            corr += coef_ref[4, j : j + 1, :] * g1 + coef_ref[5, j : j + 1, :] * g1s
-        put(8 * r, grad0, 2)
-        put(8 * r, grad1, 3)
-        corr_ref[rows] = corr
-    corr_ref[BLOCKS:] = zeros[:8]
-    after = swap(corr_ref[1 : BLOCKS + 1])
-    taps_grad = corr_ref[:BLOCKS] + jnp.where(real_lane, after, -after)
-    for r in range(BLOCKS // 8):
-        put(8 * r, taps_grad[8 * r : 8 * r + 8], 4)
+def swap(value):
+    return pltpu.roll(value, HALF, 1)
+
+
+def blocks_kernel(in_ref, there_ref, filter_there_ref, high_ref, low_ref, filter_high_ref, filter_low_ref, out_ref):
+    real = lax.broadcasted_iota(jnp.int32, (2 * BLOCKS, LANES), 1) < HALF
+
+    def spectra(table_ref, signals):
+        high, low = split(jnp.concatenate([in_ref[:, 0, LANES * s : LANES * (s + 1)] for s in signals], 1))
+        terms = dot(table_ref[...], jnp.concatenate([high, high, low], 0))
+        result = []
+        for n in range(len(signals)):
+            cols = slice(LANES * n, LANES * (n + 1))
+            sine = swap(terms[2 * BLOCKS :, cols])
+            result.append(terms[: 2 * BLOCKS, cols] + jnp.where(real, sine, -sine))
+        return result
+
+    def turn(value):
+        swapped = swap(value)
+        return jnp.where(real, -swapped, swapped)
+
+    def blocks(table_high_ref, table_low_ref, values):
+        cosine, sine = jnp.concatenate(values, 1), jnp.concatenate([turn(v) for v in values], 1)
+        high, low = split(jnp.concatenate([cosine, sine], 0))
+        table_high = table_high_ref[...]
+        return dot(table_high, high) + (dot(table_high, low) + dot(table_low_ref[...], high))
+
+    (taps,) = spectra(filter_there_ref, [4])
+    mixed0, mixed1, grad0, grad1 = spectra(there_ref, range(4))
+    taps_swap = swap(taps)
+    both_real, both_imag = jnp.where(real, taps, taps_swap), jnp.where(real, -taps_swap, taps)
+    results, corr = [], None
+    for mixed in (mixed0, mixed1):
+        results.append(both_real * mixed + both_imag * swap(mixed))
+    for mixed, grad in ((mixed0, grad0), (mixed1, grad1)):
+        grad_swap, mixed_swap = swap(grad), swap(mixed)
+        results.append(both_real * grad - both_imag * grad_swap)
+        product = jnp.where(real, mixed, mixed_swap) * grad + jnp.where(real, mixed_swap, -mixed) * grad_swap
+        corr = product if corr is None else corr + product
+    out_ref[:, 0, : 4 * LANES] = blocks(high_ref, low_ref, results)
+    out_ref[:, 0, 4 * LANES :] = blocks(filter_high_ref, filter_low_ref, [corr])
 
 
 def inverse_kernel(
@@ -206,28 +197,28 @@
     first, last, twiddle, second, second_back = jax.tree.map(jnp.asarray, make_tables())
     groups = lax.axis_size("chan")
     traffic = jax.ShapeDtypeStruct((BLOCKS, 1, WIDTH), f32)
+    vmem = pl.BlockSpec(memory_space=pltpu.VMEM)
+    operands = (gate_k, values, cotangent, gate_q, filter_taps.reshape(ROWS, LANES), first, twiddle, *second)
     sent = pl.pallas_call(
         forward_kernel,
         out_shape=traffic,
-        scratch_shapes=[pltpu.VMEM((4, ROWS, LANES), f32)],
+        in_specs=[pl.BlockSpec(memory_space=pltpu.HBM)] * len(operands),
+        scratch_shapes=[
+            *(pltpu.VMEM(v.shape, v.dtype) for v in operands),
+            pltpu.VMEM((4, ROWS, LANES), f32),
+            pltpu.SemaphoreType.DMA((len(operands),)),
+        ],
         compiler_params=SMALL,
         name="forward_transform",
-    )(gate_k, values, cotangent, gate_q, filter_taps.reshape(ROWS, LANES), first, twiddle, *second)
+    )(*operands)
     blocks = lax.all_to_all(sent, "ctx", 0, 0, tiled=True, axis_index_groups=CTX_ORDER)
     sent = pl.pallas_call(
         blocks_kernel,
         out_shape=traffic,
-        scratch_shapes=[
-            pltpu.VMEM((4, 2 * BLOCKS, LANES), f32),
-            pltpu.VMEM((4, 2 * BLOCKS, LANES), f32),
-            pltpu.VMEM((6, BLOCKS, LANES), f32),
-            pltpu.VMEM((BLOCKS + 8, LANES), f32),
-        ],
         compiler_params=SMALL,
         name="block_convolutions",
-    )(blocks)
+    )(blocks, *jax.tree.map(jnp.asarray, make_block_tables()))
     spectra = lax.all_to_all(sent, "ctx", 0, 0, tiled=True, axis_index_groups=CTX_ORDER)
-    vmem = pl.BlockSpec(memory_space=pltpu.VMEM)
     like = jax.ShapeDtypeStruct(gate_q.shape, jnp.bfloat16)
     *gated, partial_filter = pl.pallas_call(
         inverse_kernel,

time: 69.2 us -> 69 us (level)
    unnamed x36 -> x48, local copies, waits for them, and re-layouts: 6.91 us -> 6.96 us
where the time goes in v3:
time: 69 us; the launch traced here: 67.8 us
  blocking collectives  55.8 us (81%)
  local copies, waits for them, and re-layouts  6.96 us (10%)
  Pallas kernels  3.61 us (5%)
  between operations  0.85 us (1%)
    all_to_all x2, blocking collectives, per_device(): lax.all_to_all(sent, 'ctx', 0, 0, tiled=True, axis_index_groups=CTX_ORDER)  46.5 us
    all_to_all x1, blocking collectives, per_device(): lax.all_to_all(partial_filter, 'chan', 0, 0, tiled=True, axis_index_group...  9.34 us
    unnamed x48, local copies, waits for them, and re-layouts  6.96 us
    pallas_call x1, Pallas kernels, per_device(): pl.pallas_call(inverse_kernel, out_shape=(like, like, like, like, jax.Sha...  1.66 us

profile of v3, /device:TPU:1, one launch (start us, length us, event | category | flops | bytes accessed | tf_op | source)
XLA Modules:
  0.0 67.8 jit_solution(9737395918394642760)
XLA Ops:
  0.6 0.0 copy-start.22
  0.6 0.7 %copy-done.22 = bf16[64,96]{1,0:T(8,128)(2,1)S(1)} copy-done((bf16[64,96]{1,0:T(8,128)(2,1)S(1)}, bf16[64,96]{1,0:T(8,128)(2,1)}, u32[]{:S(2)}) %copy-start.22) | copy-done | bytes 12312
  1.4 0.0 copy-start.2
  1.4 0.9 %copy-done.2 = bf16[256,256]{1,0:T(8,128)(2,1)S(1)} copy-done((bf16[256,256]{1,0:T(8,128)(2,1)S(1)}, bf16[256,256]{1,0:T(8,128)(2,1)}, u32[]{:S(2)}) %copy-start.2) | copy-done | bytes 131096
  2.3 0.0 copy-start.3
  2.3 0.9 %copy-done.3 = bf16[256,256]{1,0:T(8,128)(2,1)S(1)} copy-done((bf16[256,256]{1,0:T(8,128)(2,1)S(1)}, bf16[256,256]{1,0:T(8,128)(2,1)}, u32[]{:S(2)}) %copy-start.3) | copy-done | bytes 131096
  3.2 0.0 copy-start.4
  3.2 0.8 %copy-done.4 = f32[2,32,128]{2,1,0:T(8,128)S(1)} copy-done((f32[2,32,128]{2,1,0:T(8,128)S(1)}, f32[2,32,128]{2,1,0:T(8,128)}, u32[]{:S(2)}) %copy-start.4) | copy-done | bytes 32792
  3.9 0.0 copy-start.8
  3.9 0.7 %copy-done.8 = bf16[2,4096]{1,0:T(2,128)(2,1)S(1)} copy-done((bf16[2,4096]{1,0:T(2,128)(2,1)S(1)}, bf16[2,4096]{1,0:T(2,128)(2,1)}, u32[]{:S(2)}) %copy-start.8) | copy-done | bytes 16408
  4.6 0.0 copy-start.10
  4.6 0.7 %copy-done.10 = bf16[2,4096]{1,0:T(2,128)(2,1)S(1)} copy-done((bf16[2,4096]{1,0:T(2,128)(2,1)S(1)}, bf16[2,4096]{1,0:T(2,128)(2,1)}, u32[]{:S(2)}) %copy-start.10) | copy-done | bytes 16408
  5.4 0.0 copy-start.12
  5.4 0.7 %copy-done.12 = bf16[2,4096]{1,0:T(2,128)(2,1)S(1)} copy-done((bf16[2,4096]{1,0:T(2,128)(2,1)S(1)}, bf16[2,4096]{1,0:T(2,128)(2,1)}, u32[]{:S(2)}) %copy-start.12) | copy-done | bytes 16408
  6.1 0.0 copy-start.14
  6.1 0.7 %copy-done.14 = bf16[2,4096]{1,0:T(2,128)(2,1)S(1)} copy-done((bf16[2,4096]{1,0:T(2,128)(2,1)S(1)}, bf16[2,4096]{1,0:T(2,128)(2,1)}, u32[]{:S(2)}) %copy-start.14) | copy-done | bytes 16408
  6.8 0.0 copy-start.20
  6.8 0.7 %copy-done.20 = f32[4096]{0:T(1024)S(1)} copy-done((f32[4096]{0:T(1024)S(1)}, f32[4096]{0:T(1024)}, u32[]{:S(2)}) %copy-start.20) | copy-done | bytes 16408
  7.5 0.0 copy-start.18
  7.5 0.0 copy-start.19
  7.5 1.0 %forward_transform.1 = f32[64,1,640]{2,1,0:T(1,128)S(1)} custom-call(bf16[2,4096]{1,0:T(2,128)(2,1)S(1)} %copy-done.8, bf16[2,4096]{1,0:T(2,128)(2,1)S(1)} %copy-done.10, bf16[2,4096]{1,0:T(2,128)(2,1)S(1)} %copy-done.12, bf16[2,4096]{1,0:T(2,128)(2,1)S(1)} %copy-done.14, f32[32,128]{1,0:T(8,128)S(1)} %bitcast.2, bf16[64,96]{1,0:T(8,128)(2,1)S(1)} %copy-done.22, ...), custom_call_target="tpu_custom_call" | custom-call | tf_op jit(solution)/shard_map/forward_transform/pallas_call | solution.py:202
  8.6 0.0 copy-start.6
  8.6 0.0 copy-start.7
  8.6 0.0 copy-start.16
  8.6 0.0 copy-start.17
  8.6 27.0 %all_to_all.15.in_ref = f32[64,1,640]{2,1,0:T(1,128)S(1)} all-to-all(f32[64,1,640]{2,1,0:T(1,128)S(1)} %forward_transform.1), channel_id=1, replica_groups={{416,8,16,24,32,40,48,56,64,72,80,88,96,104,112,120,128,136,144,152,160..., dimensions={0} | all-to-all | bytes 327680 | tf_op jit(solution)/shard_map/all_to_all | solution.py:214
  35.6 0.0 copy-done.18
  35.6 0.0 copy-done.19
  35.6 0.0 copy-done.6
  35.6 0.0 copy-done.7
  35.7 0.0 copy-done.16
  35.7 0.0 copy-done.17
  35.7 0.0 copy-start.13
  35.7 0.0 copy-start.15
  35.7 0.0 copy-start.21
  35.7 0.0 copy-start.23
  35.7 0.9 %block_convolutions.1 = f32[64,1,640]{2,1,0:T(1,128)S(1)} custom-call(f32[64,1,640]{2,1,0:T(1,128)S(1)} %all_to_all.15.in_ref, bf16[256,192]{1,0:T(8,128)(2,1)S(1)} %copy-done.7, bf16[256,192]{1,0:T(8,128)(2,1)S(1)} %copy-done.6, bf16[64,256]{1,0:T(8,128)(2,1)S(1)} %copy-done.19, bf16[64,256]{1,0:T(8,128)(2,1)S(1)} %copy-done.18, ...), custom_call_target="tpu_custom_call" | custom-call | tf_op jit(solution)/shard_map/block_convolutions/pallas_call | solution.py:215
  36.6 0.0 copy-start
  36.7 0.0 copy-start.1
  36.7 0.0 copy-start.5
  36.7 0.0 copy-start.9
  36.7 0.0 copy-start.11
  36.7 19.4 %all_to_all.16.in_ref = f32[64,1,640]{2,1,0:T(1,128)S(1)} all-to-all(f32[64,1,640]{2,1,0:T(1,128)S(1)} %block_convolutions.1), channel_id=1, replica_groups={{416,8,16,24,32,40,48,56,64,72,80,88,96,104,112,120,128,136,144,152,160..., dimensions={0} | all-to-all | bytes 327680 | tf_op jit(solution)/shard_map/all_to_all | solution.py:221
  56.1 0.0 copy-done.13
  56.1 0.0 copy-done.15
  56.1 0.0 copy-done.21
  56.1 0.0 copy-done.23
  56.2 0.0 copy-done
  56.2 0.0 copy-done.1
  56.2 0.0 copy-done.5
  56.2 0.0 copy-done.9
  56.2 0.0 copy-done.11
  56.2 1.7 %inverse_transform.1 = (bf16[2,4096]{1,0:T(2,128)(2,1)}, bf16[2,4096]{1,0:T(2,128)(2,1)}, bf16[2,4096]{1,0:T(2,128)(2,1)}, bf16[2,4096]{1,0:T(2,128)(2,1)}, f32[8,32,128]{2,1,0:T(8,128)S(1)}) custom-call(f32[64,1,640]{2,1,0:T(1,128)S(1)} %all_to_all.16.in_ref, bf16[2,4096]{1,0:T(2,128)(2,1)S(1)} %copy-done.15, bf16[2,4096]{1,0:T(2,128)(2,1)S(1)} %copy-done.9, ...), custom_call_target="tpu_custom_call" | custom-call | tf_op jit(solution)/shard_map/inverse_transform/pallas_call | solution.py:223
  57.9 9.3 %all_to_all.17 = f32[8,32,128]{2,1,0:T(8,128)S(1)} all-to-all(f32[8,32,128]{2,1,0:T(8,128)S(1)} %get-tuple-element.14), channel_id=1, replica_groups={{4,5,2,3,6,7,0,1},{12,13,10,11,14,15,8,9},{20,21,18,19,22,23,16,17},{28..., dimensions={0} | all-to-all | bytes 262144 | tf_op jit(solution)/shard_map/all_to_all | solution.py:231
  67.2 0.6 reduce_sum.9
Async XLA Ops:
  0.6 0.7 %copy-start.22 = (bf16[64,96]{1,0:T(8,128)(2,1)S(1)}, bf16[64,96]{1,0:T(8,128)(2,1)}, u32[]{:S(2)}) copy-start(bf16[64,96]{1,0:T(8,128)(2,1)} %constant.28.clone.refs_5_) | copy-start | bytes 36868
  1.4 0.9 %copy-start.2 = (bf16[256,256]{1,0:T(8,128)(2,1)S(1)}, bf16[256,256]{1,0:T(8,128)(2,1)}, u32[]{:S(2)}) copy-start(bf16[256,256]{1,0:T(8,128)(2,1)} %constant.32.clone.refs_8_) | copy-start | bytes 393220
  2.3 0.9 %copy-start.3 = (bf16[256,256]{1,0:T(8,128)(2,1)S(1)}, bf16[256,256]{1,0:T(8,128)(2,1)}, u32[]{:S(2)}) copy-start(bf16[256,256]{1,0:T(8,128)(2,1)} %constant.31.clone.refs_7_) | copy-start | bytes 393220
  3.2 0.8 %copy-start.4 = (f32[2,32,128]{2,1,0:T(8,128)S(1)}, f32[2,32,128]{2,1,0:T(8,128)}, u32[]{:S(2)}) copy-start(f32[2,32,128]{2,1,0:T(8,128)} %constant.30.clone.refs_6_.twiddle_ref) | copy-start | bytes 98308
  3.9 0.7 %copy-start.8 = (bf16[2,4096]{1,0:T(2,128)(2,1)S(1)}, bf16[2,4096]{1,0:T(2,128)(2,1)}, u32[]{:S(2)}) copy-start(bf16[2,4096]{1,0:T(2,128)(2,1)} %key_ref.1) | copy-start | bytes 49156
  4.6 0.7 %copy-start.10 = (bf16[2,4096]{1,0:T(2,128)(2,1)S(1)}, bf16[2,4096]{1,0:T(2,128)(2,1)}, u32[]{:S(2)}) copy-start(bf16[2,4096]{1,0:T(2,128)(2,1)} %values_ref.1) | copy-start | bytes 49156
  5.4 0.7 %copy-start.12 = (bf16[2,4096]{1,0:T(2,128)(2,1)S(1)}, bf16[2,4096]{1,0:T(2,128)(2,1)}, u32[]{:S(2)}) copy-start(bf16[2,4096]{1,0:T(2,128)(2,1)} %cot_ref.1) | copy-start | bytes 49156
  6.1 0.7 %copy-start.14 = (bf16[2,4096]{1,0:T(2,128)(2,1)S(1)}, bf16[2,4096]{1,0:T(2,128)(2,1)}, u32[]{:S(2)}) copy-start(bf16[2,4096]{1,0:T(2,128)(2,1)} %query_ref.1) | copy-start | bytes 49156
  6.8 0.7 %copy-start.20 = (f32[4096]{0:T(1024)S(1)}, f32[4096]{0:T(1024)}, u32[]{:S(2)}) copy-start(f32[4096]{0:T(1024)} %param.22) | copy-start | bytes 49156
  7.5 28.1 %copy-start.18 = (bf16[64,256]{1,0:T(8,128)(2,1)S(1)}, bf16[64,256]{1,0:T(8,128)(2,1)}, u32[]{:S(2)}) copy-start(bf16[64,256]{1,0:T(8,128)(2,1)} %constant.38.clone.low_ref) | copy-start | bytes 98308
  7.5 28.1 %copy-start.19 = (bf16[64,256]{1,0:T(8,128)(2,1)S(1)}, bf16[64,256]{1,0:T(8,128)(2,1)}, u32[]{:S(2)}) copy-start(bf16[64,256]{1,0:T(8,128)(2,1)} %constant.37.clone.high_ref) | copy-start | bytes 98308
  8.6 27.1 %copy-start.6 = (bf16[256,192]{1,0:T(8,128)(2,1)S(1)}, bf16[256,192]{1,0:T(8,128)(2,1)}, u32[]{:S(2)}) copy-start(bf16[256,192]{1,0:T(8,128)(2,1)} %constant.36.clone.filter_there_ref) | copy-start | bytes 294916
  8.6 27.1 %copy-start.7 = (bf16[256,192]{1,0:T(8,128)(2,1)S(1)}, bf16[256,192]{1,0:T(8,128)(2,1)}, u32[]{:S(2)}) copy-start(bf16[256,192]{1,0:T(8,128)(2,1)} %constant.35.clone.there_ref) | copy-start | bytes 294916
  8.6 27.1 %copy-start.16 = (bf16[64,256]{1,0:T(8,128)(2,1)S(1)}, bf16[64,256]{1,0:T(8,128)(2,1)}, u32[]{:S(2)}) copy-start(bf16[64,256]{1,0:T(8,128)(2,1)} %constant.40.clone.filter_low_ref) | copy-start | bytes 98308
  8.6 27.1 %copy-start.17 = (bf16[64,256]{1,0:T(8,128)(2,1)S(1)}, bf16[64,256]{1,0:T(8,128)(2,1)}, u32[]{:S(2)}) copy-start(bf16[64,256]{1,0:T(8,128)(2,1)} %constant.39.clone.filter_high_ref) | copy-start | bytes 98308
  35.7 20.5 %copy-start.13 = (bf16[2,4096]{1,0:T(2,128)(2,1)S(1)}, bf16[2,4096]{1,0:T(2,128)(2,1)}, u32[]{:S(2)}) copy-start(bf16[2,4096]{1,0:T(2,128)(2,1)} %cot_ref.1) | copy-start | bytes 49156
  35.7 20.5 %copy-start.15 = (bf16[2,4096]{1,0:T(2,128)(2,1)S(1)}, bf16[2,4096]{1,0:T(2,128)(2,1)}, u32[]{:S(2)}) copy-start(bf16[2,4096]{1,0:T(2,128)(2,1)} %query_ref.1) | copy-start | bytes 49156
  35.7 20.4 %copy-start.21 = (bf16[32,192]{1,0:T(8,128)(2,1)S(1)}, bf16[32,192]{1,0:T(8,128)(2,1)}, u32[]{:S(2)}) copy-start(bf16[32,192]{1,0:T(8,128)(2,1)} %constant.29.clone.last_ref) | copy-start | bytes 36868
  35.7 20.4 %copy-start.23 = (f32[2]{0:T(128)S(1)}, f32[2]{0:T(128)}, u32[]{:S(2)}) copy-start(f32[2]{0:T(128)} %gain_ref.1) | copy-start | bytes 28
  36.6 19.5 %copy-start = (bf16[256,256]{1,0:T(8,128)(2,1)S(1)}, bf16[256,256]{1,0:T(8,128)(2,1)}, u32[]{:S(2)}) copy-start(bf16[256,256]{1,0:T(8,128)(2,1)} %constant.34.clone.low_ref) | copy-start | bytes 393220
  36.7 19.5 %copy-start.1 = (bf16[256,256]{1,0:T(8,128)(2,1)S(1)}, bf16[256,256]{1,0:T(8,128)(2,1)}, u32[]{:S(2)}) copy-start(bf16[256,256]{1,0:T(8,128)(2,1)} %constant.33.clone.high_ref) | copy-start | bytes 393220
  36.7 19.5 %copy-start.5 = (f32[2,32,128]{2,1,0:T(8,128)S(1)}, f32[2,32,128]{2,1,0:T(8,128)}, u32[]{:S(2)}) copy-start(f32[2,32,128]{2,1,0:T(8,128)} %constant.30.clone.refs_6_.twiddle_ref) | copy-start | bytes 98308
  36.7 19.5 %copy-start.9 = (bf16[2,4096]{1,0:T(2,128)(2,1)S(1)}, bf16[2,4096]{1,0:T(2,128)(2,1)}, u32[]{:S(2)}) copy-start(bf16[2,4096]{1,0:T(2,128)(2,1)} %key_ref.1) | copy-start | bytes 49156
  36.7 19.5 %copy-start.11 = (bf16[2,4096]{1,0:T(2,128)(2,1)S(1)}, bf16[2,4096]{1,0:T(2,128)(2,1)}, u32[]{:S(2)}) copy-start(bf16[2,4096]{1,0:T(2,128)(2,1)} %values_ref.1) | copy-start | bytes 49156

commit v4 on v3

--- a/solution.py
+++ b/solution.py
@@ -210,7 +210,7 @@
         ],
         compiler_params=SMALL,
         name="forward_transform",
-    )(*operands)
+    )(*(pltpu.with_memory_space_constraint(v, pltpu.HBM) for v in operands))
     blocks = lax.all_to_all(sent, "ctx", 0, 0, tiled=True, axis_index_groups=CTX_ORDER)
     sent = pl.pallas_call(
         blocks_kernel,

time: 69 us -> 62.2 us (0.901)
  local copies, waits for them, and re-layouts: 6.96 us -> 0.1 us
    unnamed x48 -> x30, local copies, waits for them, and re-layouts: 6.96 us -> 0.1 us
where the time goes in v4:
time: 62.2 us; the launch traced here: 61.6 us
  blocking collectives  55.8 us (90%)
  Pallas kernels  4.21 us (7%)
  between operations  0.85 us (1%)
    all_to_all x2, blocking collectives, per_device(): lax.all_to_all(sent, 'ctx', 0, 0, tiled=True, axis_index_groups=CTX_ORDER)  46.4 us
    all_to_all x1, blocking collectives, per_device(): lax.all_to_all(partial_filter, 'chan', 0, 0, tiled=True, axis_index_group...  9.34 us
    pallas_call x1, Pallas kernels, per_device(): pl.pallas_call(inverse_kernel, out_shape=(like, like, like, like, jax.Sha...  1.66 us
    pallas_call x1, Pallas kernels, per_device(): pl.pallas_call(forward_kernel, out_shape=traffic, in_specs=[pl.BlockSpec(...  1.63 us

profile of v4, /device:TPU:1, one launch (start us, length us, event | category | flops | bytes accessed | tf_op | source)
XLA Modules:
  0.0 61.6 jit_solution(8367910528032132505)
XLA Ops:
  0.6 0.0 copy-start.11
  0.6 0.0 copy-start.12
  0.7 1.6 %forward_transform.1 = f32[64,1,640]{2,1,0:T(1,128)S(1)} custom-call(bf16[2,4096]{1,0:T(2,128)(2,1)} %key_ref.1, bf16[2,4096]{1,0:T(2,128)(2,1)} %values_ref.1, bf16[2,4096]{1,0:T(2,128)(2,1)} %cot_ref.1, bf16[2,4096]{1,0:T(2,128)(2,1)} %query_ref.1, f32[32,128]{1,0:T(8,128)} %bitcast.2, bf16[64,96]{1,0:T(8,128)(2,1)} %constant.28.clone.refs_5_, ...), custom_call_target="tpu_custom_call" | custom-call | tf_op jit(solution)/shard_map/forward_transform/pallas_call | solution.py:202
  2.3 0.0 copy-start.3
  2.3 0.0 copy-start.4
  2.3 0.0 copy-start.9
  2.3 0.0 copy-start.10
  2.3 27.0 %all_to_all.15.in_ref = f32[64,1,640]{2,1,0:T(1,128)S(1)} all-to-all(f32[64,1,640]{2,1,0:T(1,128)S(1)} %forward_transform.1), channel_id=1, replica_groups={{416,8,16,24,32,40,48,56,64,72,80,88,96,104,112,120,128,136,144,152,160..., dimensions={0} | all-to-all | bytes 327680 | tf_op jit(solution)/shard_map/all_to_all | solution.py:214
  29.4 0.0 copy-done.11
  29.4 0.0 copy-done.12
  29.4 0.0 copy-done.3
  29.4 0.0 copy-done.4
  29.4 0.0 copy-done.9
  29.4 0.0 copy-done.10
  29.4 0.0 copy-start.7
  29.4 0.0 copy-start.8
  29.4 0.0 copy-start.13
  29.4 0.0 copy-start.14
  29.5 0.9 %block_convolutions.1 = f32[64,1,640]{2,1,0:T(1,128)S(1)} custom-call(f32[64,1,640]{2,1,0:T(1,128)S(1)} %all_to_all.15.in_ref, bf16[256,192]{1,0:T(8,128)(2,1)S(1)} %copy-done.4, bf16[256,192]{1,0:T(8,128)(2,1)S(1)} %copy-done.3, bf16[64,256]{1,0:T(8,128)(2,1)S(1)} %copy-done.12, bf16[64,256]{1,0:T(8,128)(2,1)S(1)} %copy-done.11, ...), custom_call_target="tpu_custom_call" | custom-call | tf_op jit(solution)/shard_map/block_convolutions/pallas_call | solution.py:215
  30.4 0.0 copy-start
  30.4 0.0 copy-start.1
  30.4 0.0 copy-start.2
  30.4 0.0 copy-start.5
  30.4 0.0 copy-start.6
  30.4 19.4 %all_to_all.16.in_ref = f32[64,1,640]{2,1,0:T(1,128)S(1)} all-to-all(f32[64,1,640]{2,1,0:T(1,128)S(1)} %block_convolutions.1), channel_id=1, replica_groups={{416,8,16,24,32,40,48,56,64,72,80,88,96,104,112,120,128,136,144,152,160..., dimensions={0} | all-to-all | bytes 327680 | tf_op jit(solution)/shard_map/all_to_all | solution.py:221
  49.9 0.0 copy-done.7
  49.9 0.0 copy-done.8
  49.9 0.0 copy-done.13
  49.9 0.0 copy-done.14
  49.9 0.0 copy-done
  49.9 0.0 copy-done.1
  49.9 0.0 copy-done.2
  49.9 0.0 copy-done.5
  49.9 0.0 copy-done.6
  49.9 1.7 %inverse_transform.1 = (bf16[2,4096]{1,0:T(2,128)(2,1)}, bf16[2,4096]{1,0:T(2,128)(2,1)}, bf16[2,4096]{1,0:T(2,128)(2,1)}, bf16[2,4096]{1,0:T(2,128)(2,1)}, f32[8,32,128]{2,1,0:T(8,128)S(1)}) custom-call(f32[64,1,640]{2,1,0:T(1,128)S(1)} %all_to_all.16.in_ref, bf16[2,4096]{1,0:T(2,128)(2,1)S(1)} %copy-done.8, bf16[2,4096]{1,0:T(2,128)(2,1)S(1)} %copy-done.5, ...), custom_call_target="tpu_custom_call" | custom-call | tf_op jit(solution)/shard_map/inverse_transform/pallas_call | solution.py:223
  51.6 9.3 %all_to_all.17 = f32[8,32,128]{2,1,0:T(8,128)S(1)} all-to-all(f32[8,32,128]{2,1,0:T(8,128)S(1)} %get-tuple-element.14), channel_id=1, replica_groups={{4,5,2,3,6,7,0,1},{12,13,10,11,14,15,8,9},{20,21,18,19,22,23,16,17},{28..., dimensions={0} | all-to-all | bytes 262144 | tf_op jit(solution)/shard_map/all_to_all | solution.py:231
  60.9 0.6 %reduce_sum.9 = f32[32,128]{1,0:T(8,128)} reduce(f32[8,32,128]{2,1,0:T(8,128)S(1)} %all_to_all.17, f32[]{:T(128)} %constant.13.clone.1), dimensions={0}, to_apply=%region_0.0 | reduce | flops 28672 | bytes 147460 | tf_op jit(solution)/shard_map/reduce_sum | solution.py:231
Async XLA Ops:
  0.6 28.7 %copy-start.11 = (bf16[64,256]{1,0:T(8,128)(2,1)S(1)}, bf16[64,256]{1,0:T(8,128)(2,1)}, u32[]{:S(2)}) copy-start(bf16[64,256]{1,0:T(8,128)(2,1)} %constant.38.clone.low_ref) | copy-start | bytes 98308
  0.6 28.7 %copy-start.12 = (bf16[64,256]{1,0:T(8,128)(2,1)S(1)}, bf16[64,256]{1,0:T(8,128)(2,1)}, u32[]{:S(2)}) copy-start(bf16[64,256]{1,0:T(8,128)(2,1)} %constant.37.clone.high_ref) | copy-start | bytes 98308
  2.3 27.1 %copy-start.3 = (bf16[256,192]{1,0:T(8,128)(2,1)S(1)}, bf16[256,192]{1,0:T(8,128)(2,1)}, u32[]{:S(2)}) copy-start(bf16[256,192]{1,0:T(8,128)(2,1)} %constant.36.clone.filter_there_ref) | copy-start | bytes 294916
  2.3 27.1 %copy-start.4 = (bf16[256,192]{1,0:T(8,128)(2,1)S(1)}, bf16[256,192]{1,0:T(8,128)(2,1)}, u32[]{:S(2)}) copy-start(bf16[256,192]{1,0:T(8,128)(2,1)} %constant.35.clone.there_ref) | copy-start | bytes 294916
  2.3 27.1 %copy-start.9 = (bf16[64,256]{1,0:T(8,128)(2,1)S(1)}, bf16[64,256]{1,0:T(8,128)(2,1)}, u32[]{:S(2)}) copy-start(bf16[64,256]{1,0:T(8,128)(2,1)} %constant.40.clone.filter_low_ref) | copy-start | bytes 98308
  2.3 27.1 %copy-start.10 = (bf16[64,256]{1,0:T(8,128)(2,1)S(1)}, bf16[64,256]{1,0:T(8,128)(2,1)}, u32[]{:S(2)}) copy-start(bf16[64,256]{1,0:T(8,128)(2,1)} %constant.39.clone.filter_high_ref) | copy-start | bytes 98308
  29.4 20.5 %copy-start.7 = (bf16[2,4096]{1,0:T(2,128)(2,1)S(1)}, bf16[2,4096]{1,0:T(2,128)(2,1)}, u32[]{:S(2)}) copy-start(bf16[2,4096]{1,0:T(2,128)(2,1)} %cot_ref.1) | copy-start | bytes 49156
  29.4 20.5 %copy-start.8 = (bf16[2,4096]{1,0:T(2,128)(2,1)S(1)}, bf16[2,4096]{1,0:T(2,128)(2,1)}, u32[]{:S(2)}) copy-start(bf16[2,4096]{1,0:T(2,128)(2,1)} %query_ref.1) | copy-start | bytes 49156
  29.4 20.4 %copy-start.13 = (bf16[32,192]{1,0:T(8,128)(2,1)S(1)}, bf16[32,192]{1,0:T(8,128)(2,1)}, u32[]{:S(2)}) copy-start(bf16[32,192]{1,0:T(8,128)(2,1)} %constant.29.clone.last_ref) | copy-start | bytes 36868
  29.4 20.4 %copy-start.14 = (f32[2]{0:T(128)S(1)}, f32[2]{0:T(128)}, u32[]{:S(2)}) copy-start(f32[2]{0:T(128)} %gain_ref.1) | copy-start | bytes 28
  30.4 19.5 %copy-start = (bf16[256,256]{1,0:T(8,128)(2,1)S(1)}, bf16[256,256]{1,0:T(8,128)(2,1)}, u32[]{:S(2)}) copy-start(bf16[256,256]{1,0:T(8,128)(2,1)} %constant.34.clone.low_ref) | copy-start | bytes 393220
  30.4 19.5 %copy-start.1 = (bf16[256,256]{1,0:T(8,128)(2,1)S(1)}, bf16[256,256]{1,0:T(8,128)(2,1)}, u32[]{:S(2)}) copy-start(bf16[256,256]{1,0:T(8,128)(2,1)} %constant.33.clone.high_ref) | copy-start | bytes 393220
  30.4 19.5 %copy-start.2 = (f32[2,32,128]{2,1,0:T(8,128)S(1)}, f32[2,32,128]{2,1,0:T(8,128)}, u32[]{:S(2)}) copy-start(f32[2,32,128]{2,1,0:T(8,128)} %constant.30.clone.refs_6_.twiddle_ref) | copy-start | bytes 98308
  30.4 19.5 %copy-start.5 = (bf16[2,4096]{1,0:T(2,128)(2,1)S(1)}, bf16[2,4096]{1,0:T(2,128)(2,1)}, u32[]{:S(2)}) copy-start(bf16[2,4096]{1,0:T(2,128)(2,1)} %key_ref.1) | copy-start | bytes 49156
  30.4 19.5 %copy-start.6 = (bf16[2,4096]{1,0:T(2,128)(2,1)S(1)}, bf16[2,4096]{1,0:T(2,128)(2,1)}, u32[]{:S(2)}) copy-start(bf16[2,4096]{1,0:T(2,128)(2,1)} %values_ref.1) | copy-start | bytes 49156

commit v5 on v4

v5 whole, which is shorter than its diff:
```python
import numpy as np

import jax
import jax.numpy as jnp
from jax import lax
from jax.experimental import pallas as pl
from jax.experimental.pallas import tpu as pltpu
from jax.sharding import PartitionSpec as P

BLOCK = 4096
BLOCKS = 64
ROWS = 32
LANES = 128
HALVES = 32
SIGNALS = 5
PAIR = 2 * LANES
WIDTH = SIGNALS * PAIR
SMALL = pltpu.CompilerParams(vmem_limit_bytes=8 << 20)
CORNER = 20
PLANE_ORDER = [CORNER if p == 0 else 0 if p == CORNER else p for p in range(HALVES)]
CTX_ORDER = [[HALVES + p for p in PLANE_ORDER] + PLANE_ORDER]
HALF_ORDER = [PLANE_ORDER, [HALVES + p for p in PLANE_ORDER]]
CHAN_ORDER = [[5, 4, 2, 3, 6, 7, 0, 1]]


def split(value):
    high = value.astype(jnp.bfloat16)
    return high, (value - high.astype(jnp.float32)).astype(jnp.bfloat16)


def split_table(table):
    high = table.astype(np.float32).astype(jnp.bfloat16)
    low = (table - high.astype(np.float64)).astype(np.float32).astype(jnp.bfloat16)
    return high, low


def make_tables():
    a = np.arange(ROWS)
    b = np.arange(LANES)
    first = np.exp(-2j * np.pi * (a[:, None] * a[None, :] / ROWS + LANES * a[None, :] / (4 * BLOCK)))
    first = np.concatenate([first.real, first.imag], 0)
    first_pair = np.zeros((2, 2 * ROWS, ROWS, 2))
    first_pair[0, :, :, 0] = first_pair[1, :, :, 1] = first
    last = np.exp(2j * np.pi * (a[:, None] * a[None, :] / ROWS + LANES * a[:, None] / (4 * BLOCK)))
    last = np.concatenate([last.real, -last.imag], 1) / BLOCK / (BLOCK * BLOCKS) ** 0.5
    last_pair = np.zeros((ROWS, 2, 2, 2 * ROWS))
    last_pair[:, 0, 0] = last_pair[:, 1, 1] = last

    def thrice(table):
        high, low = split_table(table)
        return np.concatenate([high, low, high], 1)

    first_table = thrice(first_pair.reshape(4 * ROWS, 2 * ROWS)), thrice(first)
    last_table = thrice(last_pair.reshape(2 * ROWS, 4 * ROWS)), thrice(last)
    twiddle = np.exp(-2j * np.pi * b[None, :] * (4 * a[:, None] + 1) / (4 * BLOCK))
    twiddle = np.stack([twiddle.real, twiddle.imag]).astype(np.float32)
    angle = 2 * np.pi * (b[:, None] * b[None, :] % LANES) / LANES
    cos, sin = np.cos(angle), np.sin(angle)
    second = np.block([[cos, -sin], [sin, cos]])
    return first_table, last_table, twiddle, split_table(second), split_table(second.T)


def make_block_tables():
    blocks = np.array(CTX_ORDER[0])
    phases = np.arange(2 * BLOCKS)
    wave = np.exp(-2j * np.pi * phases[:, None] * blocks[None, :] / (2 * BLOCKS))
    step = np.exp(-2j * np.pi * phases / (2 * BLOCKS))
    back = np.conj(wave.T) / (2 * BLOCKS)

    def there(table):
        high, low = split_table(np.concatenate([table.real, -table.imag], 0))
        return np.concatenate([high, low, high], 1)

    def here(table):
        rows = [table[HALVES:], table[:HALVES]]
        return split_table(np.stack([np.concatenate([t.real, t.imag], 1) for t in rows]))

    filter_wave = wave * (1 + 1j * step)[:, None]
    filter_back = back * (1 - 1j * np.conj(step))[None, :]
    return there(wave), there(filter_wave), *here(back), *here(filter_back)


def dot(left, right):
    return jnp.dot(left, right, preferred_element_type=jnp.float32)


def dot3(value, high, low):
    value_high, value_low = split(value)
    rows = value.shape[0]
    both = dot(jnp.concatenate([value_high, value_low], 0), high)
    return both[:rows] + (dot(value_high, low) + both[rows:])


def stack3(value):
    high, low = split(value)
    return jnp.concatenate([high, high, low], 0)


def forward_kernel(*refs):
    operands, (out_ref, *held, sems) = refs[:10], refs[10:]
    copies = [pltpu.make_async_copy(src, dst, sems.at[n]) for n, (src, dst) in enumerate(zip(operands, held))]
    for copy in copies:
        copy.start()
    key_ref, values_ref, cot_ref, query_ref, taps_ref, pair_ref, first_ref, twiddle_ref, high_ref, low_ref = held
    f32 = jnp.float32
    for copy in copies[:5]:
        copy.wait()
    mixed = key_ref[...].astype(f32) * values_ref[...].astype(f32)
    grad = cot_ref[...].astype(f32) * query_ref[...].astype(f32)
    pairs, taps = stack3(jnp.concatenate([mixed, grad], 1)), stack3(taps_ref[...])
    for copy in copies[5:7]:
        copy.wait()
    pairs, taps = dot(pair_ref[...], pairs), dot(first_ref[...], taps)
    copies[7].wait()
    tw_re, tw_im = twiddle_ref[0], twiddle_ref[1]
    places = [(pairs, 0, 0), (pairs, 1, 0), (pairs, 0, 1), (pairs, 1, 1), (taps, 0, 0)]
    turned = []
    for spread, row, col in places:
        cols = slice(LANES * col, LANES * (col + 1))
        re = spread[2 * ROWS * row : 2 * ROWS * row + ROWS, cols]
        im = spread[2 * ROWS * row + ROWS : 2 * ROWS * (row + 1), cols]
        turned.append(jnp.concatenate([re * tw_re - im * tw_im, re * tw_im + im * tw_re], 1))
    for copy in copies[8:]:
        copy.wait()
    spectra = dot3(jnp.concatenate(turned, 0), high_ref[...], low_ref[...])
    for s in range(SIGNALS):
        for h in range(2):
            out_ref[HALVES * h : HALVES * (h + 1), 0, PAIR * s : PAIR * (s + 1)] = spectra[ROWS * s : ROWS * (s + 1)]


def blocks_kernel(in_ref, there_ref, filter_there_ref, high_ref, low_ref, filter_high_ref, filter_low_ref, out_ref):
    half = lax.axis_index("ctx") // HALVES

    def spectra(table_ref, signals):
        high, low = split(jnp.concatenate([in_ref[:, 0, PAIR * s : PAIR * (s + 1)] for s in signals], 1))
        terms = dot(table_ref[...], jnp.concatenate([high, high, low], 0))
        cosine, sine = terms[: 2 * BLOCKS], terms[2 * BLOCKS :]
        result = []
        for n in range(len(signals)):
            real, imag = slice(PAIR * n, PAIR * n + LANES), slice(PAIR * n + LANES, PAIR * (n + 1))
            result.append((cosine[:, real] + sine[:, imag], cosine[:, imag] - sine[:, real]))
        return result

    def blocks(table_high_ref, table_low_ref, values):
        cosine = jnp.concatenate([part for real, imag in values for part in (real, imag)], 1)
        sine = jnp.concatenate([part for real, imag in values for part in (-imag, real)], 1)
        high, low = split(jnp.concatenate([cosine, sine], 0))
        table_high = table_high_ref[half]
        both = dot(jnp.concatenate([table_high, table_low_ref[half]], 0), high)
        return both[:HALVES] + (dot(table_high, low) + both[HALVES:])

    ((taps_re, taps_im),) = spectra(filter_there_ref, [4])
    signals = spectra(there_ref, range(4))
    results, corr_re, corr_im = [], 0.0, 0.0
    for re, im in signals[:2]:
        results.append((taps_re * re - taps_im * im, taps_re * im + taps_im * re))
    for (mixed_re, mixed_im), (re, im) in zip(signals[:2], signals[2:]):
        results.append((taps_re * re + taps_im * im, taps_re * im - taps_im * re))
        corr_re += mixed_re * re + mixed_im * im
        corr_im += mixed_re * im - mixed_im * re
    out_ref[:, 0, : 4 * PAIR] = blocks(high_ref, low_ref, results)
    out_ref[:, 0, 4 * PAIR :] = blocks(filter_high_ref, filter_low_ref, [(corr_re, corr_im)])


def inverse_kernel(
    in_ref, query_ref, key_ref, values_ref, cot_ref, gain_ref, pair_ref, last_ref, twiddle_ref, high_ref, low_ref,
    out_ref, grad_query_ref, grad_key_ref, grad_values_ref, grad_filter_ref,
):
    f32, bf16 = jnp.float32, jnp.bfloat16
    spectra = jnp.concatenate([in_ref[:, 0, PAIR * s : PAIR * (s + 1)] for s in range(SIGNALS)], 0)
    spread = dot3(spectra, high_ref[...], low_ref[...])
    tw_re, tw_im = twiddle_ref[0], twiddle_ref[1]
    turned = []
    for s in range(SIGNALS):
        rows = slice(ROWS * s, ROWS * (s + 1))
        re, im = spread[rows, :LANES], spread[rows, LANES:]
        turned += [re * tw_re + im * tw_im, im * tw_re - re * tw_im]
    pairs = jnp.concatenate([jnp.concatenate(turned[:4], 0), jnp.concatenate(turned[4:8], 0)], 1)
    grad_filter = dot(last_ref[...], stack3(jnp.concatenate(turned[8:], 0)))
    for copy in range(grad_filter_ref.shape[0]):
        grad_filter_ref[copy] = grad_filter
    pairs = dot(pair_ref[...], stack3(pairs))
    query, cot = query_ref[...].astype(f32), cot_ref[...].astype(f32)
    key, value = key_ref[...].astype(f32), values_ref[...].astype(f32)
    first_channel = lax.broadcasted_iota(jnp.int32, query.shape, 0) % 2 == 0
    gain = jnp.where(first_channel, gain_ref[0], gain_ref[1])
    summed = pairs[:, :LANES] + gain * (key * value)
    out_ref[...] = (query * summed).astype(bf16)
    grad_query_ref[...] = (cot * summed).astype(bf16)
    grad_mixed = pairs[:, LANES:] + gain * (cot * query)
    grad_key_ref[...] = (grad_mixed * value).astype(bf16)
    grad_values_ref[...] = (grad_mixed * key).astype(bf16)


def by_rows(pair):
    return pair.reshape(2, ROWS, LANES).transpose(1, 0, 2).reshape(2 * ROWS, LANES)


def by_channel(rows):
    return rows.reshape(ROWS, 2, LANES).transpose(1, 0, 2).reshape(2, BLOCK)


def per_device(gate_q, gate_k, values, filter_taps, skip_gain, cotangent):
    f32 = jnp.float32
    first, last, twiddle, second, second_back = jax.tree.map(jnp.asarray, make_tables())
    groups = lax.axis_size("chan")
    gate_q, gate_k, values, cotangent = map(by_rows, (gate_q, gate_k, values, cotangent))
    vmem = pl.BlockSpec(memory_space=pltpu.VMEM)
    operands = (gate_k, values, cotangent, gate_q, filter_taps.reshape(ROWS, LANES), *first, twiddle, *second)
    sent = pl.pallas_call(
        forward_kernel,
        out_shape=jax.ShapeDtypeStruct((BLOCKS, 1, WIDTH), f32),
        in_specs=[pl.BlockSpec(memory_space=pltpu.HBM)] * len(operands),
        scratch_shapes=[
            *(pltpu.VMEM(v.shape, v.dtype) for v in operands),
            pltpu.SemaphoreType.DMA((len(operands),)),
        ],
        compiler_params=SMALL,
        name="forward_transform",
    )(*(pltpu.with_memory_space_constraint(v, pltpu.HBM) for v in operands))
    blocks = lax.all_to_all(sent, "ctx", 0, 0, tiled=True, axis_index_groups=CTX_ORDER)
    sent = pl.pallas_call(
        blocks_kernel,
        out_shape=jax.ShapeDtypeStruct((HALVES, 1, WIDTH), f32),
        compiler_params=SMALL,
        name="block_convolutions",
    )(blocks, *jax.tree.map(jnp.asarray, make_block_tables()))
    spectra = lax.all_to_all(sent, "ctx", 0, 0, tiled=True, axis_index_groups=HALF_ORDER)
    like = jax.ShapeDtypeStruct(gate_q.shape, jnp.bfloat16)
    *gated, partial_filter = pl.pallas_call(
        inverse_kernel,
        out_shape=(like, like, like, like, jax.ShapeDtypeStruct((groups, ROWS, LANES), f32)),
        in_specs=[vmem] * 5 + [pl.BlockSpec(memory_space=pltpu.SMEM)] + [vmem] * 5,
        compiler_params=SMALL,
        name="inverse_transform",
    )(spectra, gate_q, gate_k, values, cotangent, skip_gain, *last, twiddle, *second_back)
    partials = lax.all_to_all(partial_filter, "chan", 0, 0, tiled=True, axis_index_groups=CHAN_ORDER)
    grad_filter = jnp.sum(partials, axis=0)
    return (*map(by_channel, gated), grad_filter.reshape(BLOCK))


def solution(mesh):
    return jax.shard_map(
        per_device,
        mesh=mesh,
        in_specs=(
            P("chan", "ctx"),
            P("chan", "ctx"),
            P("chan", "ctx"),
            P("ctx"),
            P("chan"),
            P("chan", "ctx"),
        ),
        out_specs=(
            P("chan", "ctx"),
            P("chan", "ctx"),
            P("chan", "ctx"),
            P("chan", "ctx"),
            P("ctx"),
        ),
        check_vma=False,
    )
```

time: 62.2 us -> 60.6 us (0.974)
  blocking collectives: 55.8 us -> 54.7 us
    all_to_all x2 -> x1, blocking collectives: 46.4 us -> 31 us  [per_device(): lax.all_to_all(sent, 'ctx', 0, 0, tiled=True, axis_index_groups=CTX_ORDER)]
    all_to_all x0 -> x1, blocking collectives: none -> 14.1 us  [per_device(): lax.all_to_all(sent, 'ctx', 0, 0, tiled=True, axis_index_groups=HALF_ORDER)]
where the time goes in v5:
time: 60.6 us; the launch traced here: 60.3 us
  blocking collectives  54.7 us (90%)
  Pallas kernels  4 us (7%)
  between operations  0.86 us (1%)
  other arithmetic  0.62 us (1%)
    all_to_all x1, blocking collectives, per_device(): lax.all_to_all(sent, 'ctx', 0, 0, tiled=True, axis_index_groups=CTX_ORDER)  31 us
    all_to_all x1, blocking collectives, per_device(): lax.all_to_all(sent, 'ctx', 0, 0, tiled=True, axis_index_groups=HALF_ORDER)  14.1 us
    all_to_all x1, blocking collectives, per_device(): lax.all_to_all(partial_filter, 'chan', 0, 0, tiled=True, axis_index_group...  9.72 us
    pallas_call x1, Pallas kernels, per_device(): pl.pallas_call(inverse_kernel, out_shape=(like, like, like, like, jax.Sha...  1.64 us
    pallas_call x1, Pallas kernels, per_device(): pl.pallas_call(forward_kernel, out_shape=jax.ShapeDtypeStruct((BLOCKS, 1,...  1.51 us

profile of v5, /device:TPU:1, one launch (start us, length us, event | category | flops | bytes accessed | tf_op | source)
XLA Modules:
  0.0 60.3 jit_solution(322253951752203860)
XLA Ops:
  0.6 1.5 %forward_transform.1 = f32[64,1,1280]{2,1,0:T(1,128)S(1)} custom-call(bf16[64,128]{1,0:T(8,128)(2,1)} %bitcast.42, bf16[64,128]{1,0:T(8,128)(2,1)} %bitcast.44, bf16[64,128]{1,0:T(8,128)(2,1)} %bitcast.46, bf16[64,128]{1,0:T(8,128)(2,1)} %bitcast.48, f32[32,128]{1,0:T(8,128)} %bitcast.50, bf16[128,192]{1,0:T(8,128)(2,1)} %constant.32.clone.refs_5_, ...), custom_call_target="tpu_custom_call" | custom-call | tf_op jit(solution)/shard_map/forward_transform/pallas_call | solution.py:210
  2.1 0.0 copy-start
  2.2 0.0 copy-start.1
  2.2 0.0 copy-start.10
  2.2 0.0 copy-start.11
  2.2 0.0 copy-start.12
  2.2 0.0 copy-start.13
  2.2 31.0 %all_to_all.15.in_ref = f32[64,1,1280]{2,1,0:T(1,128)S(1)} all-to-all(f32[64,1,1280]{2,1,0:T(1,128)S(1)} %forward_transform.1), channel_id=1, replica_groups={{416,264,272,280,288,296,304,312,320,328,336,344,352,360,368,376,384,39..., dimensions={0} | all-to-all | bytes 655360 | tf_op jit(solution)/shard_map/all_to_all | solution.py:221
  33.2 0.0 copy-done
  33.2 0.0 copy-done.1
  33.2 0.0 copy-done.10
  33.2 0.0 copy-done.11
  33.2 0.0 copy-done.12
  33.2 0.0 copy-done.13
  33.2 0.0 copy-start.7
  33.2 0.0 copy-start.8
  33.2 0.0 copy-start.9
  33.3 0.0 copy-start.14
  33.3 0.0 copy-start.15
  33.3 0.9 %block_convolutions.1 = f32[32,1,1280]{2,1,0:T(1,128)S(1)} custom-call(f32[64,1,1280]{2,1,0:T(1,128)S(1)} %all_to_all.15.in_ref, bf16[256,192]{1,0:T(8,128)(2,1)S(1)} %copy-done.1, bf16[256,192]{1,0:T(8,128)(2,1)S(1)} %copy-done, bf16[2,32,256]{2,1,0:T(8,128)(2,1)S(1)} %copy-done.13, bf16[2,32,256]{2,1,0:T(8,128)(2,1)S(1)} %copy-done.12, ...), custom_call_target="tpu_custom_call" | custom-call | tf_op jit(solution)/shard_map/block_convolutions/pallas_call | solution.py:222
  34.2 0.0 copy-start.2
  34.2 0.0 copy-start.3
  34.2 0.0 copy-start.4
  34.2 0.0 copy-start.5
  34.2 0.0 copy-start.6
  34.2 14.1 %all_to_all.16.in_ref = f32[32,1,1280]{2,1,0:T(1,128)S(1)} all-to-all(f32[32,1,1280]{2,1,0:T(1,128)S(1)} %block_convolutions.1), channel_id=1, replica_groups={{160,8,16,24,32,40,48,56,64,72,80,88,96,104,112,120,128,136,144,152,0,1..., dimensions={0} | all-to-all | bytes 327680 | tf_op jit(solution)/shard_map/all_to_all | solution.py:228
  48.3 0.0 copy-done.7
  48.3 0.0 copy-done.8
  48.3 0.0 copy-done.9
  48.3 0.0 copy-done.14
  48.3 0.0 copy-done.15
  48.3 0.0 copy-done.2
  48.3 0.0 copy-done.3
  48.3 0.0 copy-done.4
  48.3 0.0 copy-done.5
  48.3 0.0 copy-done.6
  48.4 1.6 %inverse_transform.1 = (bf16[64,128]{1,0:T(8,128)(2,1)}, bf16[64,128]{1,0:T(8,128)(2,1)}, bf16[64,128]{1,0:T(8,128)(2,1)}, bf16[64,128]{1,0:T(8,128)(2,1)}, f32[8,32,128]{2,1,0:T(8,128)S(1)}) custom-call(f32[32,1,1280]{2,1,0:T(1,128)S(1)} %all_to_all.16.in_ref, bf16[64,128]{1,0:T(8,128)(2,1)S(1)} %bitcast.49, bf16[64,128]{1,0:T(8,128)(2,1)S(1)} %bitcast.43, ...), custom_call_target="tpu_custom_call" | custom-call | tf_op jit(solution)/shard_map/inverse_transform/pallas_call | solution.py:230
  50.0 9.7 %all_to_all.17 = f32[8,32,128]{2,1,0:T(8,128)S(1)} all-to-all(f32[8,32,128]{2,1,0:T(8,128)S(1)} %get-tuple-element.14), channel_id=1, replica_groups={{5,4,2,3,6,7,0,1},{13,12,10,11,14,15,8,9},{21,20,18,19,22,23,16,17},{29..., dimensions={0} | all-to-all | bytes 262144 | tf_op jit(solution)/shard_map/all_to_all | solution.py:237
  59.7 0.6 %reduce_sum.9 = f32[32,128]{1,0:T(8,128)} reduce(f32[8,32,128]{2,1,0:T(8,128)S(1)} %all_to_all.17, f32[]{:T(128)} %constant.15.clone.1), dimensions={0}, to_apply=%region_0.0 | reduce | flops 28672 | bytes 147460 | tf_op jit(solution)/shard_map/reduce_sum | solution.py:238
Async XLA Ops:
  2.1 31.0 %copy-start = (bf16[256,192]{1,0:T(8,128)(2,1)S(1)}, bf16[256,192]{1,0:T(8,128)(2,1)}, u32[]{:S(2)}) copy-start(bf16[256,192]{1,0:T(8,128)(2,1)} %constant.42.clone.filter_there_ref) | copy-start | bytes 294916
  2.2 31.0 %copy-start.1 = (bf16[256,192]{1,0:T(8,128)(2,1)S(1)}, bf16[256,192]{1,0:T(8,128)(2,1)}, u32[]{:S(2)}) copy-start(bf16[256,192]{1,0:T(8,128)(2,1)} %constant.41.clone.there_ref) | copy-start | bytes 294916
  2.2 31.0 %copy-start.10 = (bf16[2,32,256]{2,1,0:T(8,128)(2,1)S(1)}, bf16[2,32,256]{2,1,0:T(8,128)(2,1)}, u32[]{:S(2)}) copy-start(bf16[2,32,256]{2,1,0:T(8,128)(2,1)} %constant.46.clone.filter_low_ref) | copy-start | bytes 98308
  2.2 31.0 %copy-start.11 = (bf16[2,32,256]{2,1,0:T(8,128)(2,1)S(1)}, bf16[2,32,256]{2,1,0:T(8,128)(2,1)}, u32[]{:S(2)}) copy-start(bf16[2,32,256]{2,1,0:T(8,128)(2,1)} %constant.45.clone.filter_high_ref) | copy-start | bytes 98308
  2.2 31.0 %copy-start.12 = (bf16[2,32,256]{2,1,0:T(8,128)(2,1)S(1)}, bf16[2,32,256]{2,1,0:T(8,128)(2,1)}, u32[]{:S(2)}) copy-start(bf16[2,32,256]{2,1,0:T(8,128)(2,1)} %constant.44.clone.low_ref) | copy-start | bytes 98308
  2.2 31.0 %copy-start.13 = (bf16[2,32,256]{2,1,0:T(8,128)(2,1)S(1)}, bf16[2,32,256]{2,1,0:T(8,128)(2,1)}, u32[]{:S(2)}) copy-start(bf16[2,32,256]{2,1,0:T(8,128)(2,1)} %constant.43.clone.high_ref) | copy-start | bytes 98308
  33.2 15.0 %copy-start.7 = (bf16[2,4096]{1,0:T(2,128)(2,1)S(1)}, bf16[2,4096]{1,0:T(2,128)(2,1)}, u32[]{:S(2)}) copy-start(bf16[2,4096]{1,0:T(2,128)(2,1)} %param.26) | copy-start | bytes 49156
  33.2 15.0 %copy-start.8 = (bf16[2,4096]{1,0:T(2,128)(2,1)S(1)}, bf16[2,4096]{1,0:T(2,128)(2,1)}, u32[]{:S(2)}) copy-start(bf16[2,4096]{1,0:T(2,128)(2,1)} %param.21) | copy-start | bytes 49156
  33.2 15.0 %copy-start.9 = (bf16[64,384]{1,0:T(8,128)(2,1)S(1)}, bf16[64,384]{1,0:T(8,128)(2,1)}, u32[]{:S(2)}) copy-start(bf16[64,384]{1,0:T(8,128)(2,1)} %constant.34.clone.pair_ref) | copy-start | bytes 147460
  33.3 15.0 %copy-start.14 = (bf16[32,192]{1,0:T(8,128)(2,1)S(1)}, bf16[32,192]{1,0:T(8,128)(2,1)}, u32[]{:S(2)}) copy-start(bf16[32,192]{1,0:T(8,128)(2,1)} %constant.35.clone.last_ref) | copy-start | bytes 36868
  33.3 15.0 %copy-start.15 = (f32[2]{0:T(128)S(1)}, f32[2]{0:T(128)}, u32[]{:S(2)}) copy-start(f32[2]{0:T(128)} %gain_ref.1) | copy-start | bytes 28
  34.2 14.2 %copy-start.2 = (bf16[256,256]{1,0:T(8,128)(2,1)S(1)}, bf16[256,256]{1,0:T(8,128)(2,1)}, u32[]{:S(2)}) copy-start(bf16[256,256]{1,0:T(8,128)(2,1)} %constant.40.clone.low_ref) | copy-start | bytes 393220
  34.2 14.1 %copy-start.3 = (bf16[256,256]{1,0:T(8,128)(2,1)S(1)}, bf16[256,256]{1,0:T(8,128)(2,1)}, u32[]{:S(2)}) copy-start(bf16[256,256]{1,0:T(8,128)(2,1)} %constant.39.clone.high_ref) | copy-start | bytes 393220
  34.2 14.1 %copy-start.4 = (f32[2,32,128]{2,1,0:T(8,128)S(1)}, f32[2,32,128]{2,1,0:T(8,128)}, u32[]{:S(2)}) copy-start(f32[2,32,128]{2,1,0:T(8,128)} %constant.36.clone.refs_7_.twiddle_ref) | copy-start | bytes 98308
  34.2 14.1 %copy-start.5 = (bf16[2,4096]{1,0:T(2,128)(2,1)S(1)}, bf16[2,4096]{1,0:T(2,128)(2,1)}, u32[]{:S(2)}) copy-start(bf16[2,4096]{1,0:T(2,128)(2,1)} %param.22) | copy-start | bytes 49156
  34.2 14.1 %copy-start.6 = (bf16[2,4096]{1,0:T(2,128)(2,1)S(1)}, bf16[2,4096]{1,0:T(2,128)(2,1)}, u32[]{:S(2)}) copy-start(bf16[2,4096]{1,0:T(2,128)(2,1)} %param.23) | copy-start | bytes 49156

commit v6 on v5

--- a/solution.py
+++ b/solution.py
@@ -132,7 +132,8 @@
     half = lax.axis_index("ctx") // HALVES
 
     def spectra(table_ref, signals):
-        high, low = split(jnp.concatenate([in_ref[:, 0, PAIR * s : PAIR * (s + 1)] for s in signals], 1))
+        cols = slice(PAIR * signals[0], PAIR * (signals[-1] + 1))
+        high, low = split(jnp.concatenate([in_ref[n : n + 16, 0, cols] for n in range(0, BLOCKS, 16)], 0))
         terms = dot(table_ref[...], jnp.concatenate([high, high, low], 0))
         cosine, sine = terms[: 2 * BLOCKS], terms[2 * BLOCKS :]
         result = []
@@ -192,6 +193,17 @@
     grad_values_ref[...] = (grad_mixed * key).astype(bf16)
 
 
+def finish_kernel(partials_ref, *refs):
+    gated, outs, (total_ref, sems) = refs[:4], refs[4:9], refs[9:]
+    copies = [pltpu.make_async_copy(src, dst, sems.at[n]) for n, (src, dst) in enumerate(zip((*gated, total_ref), outs))]
+    for copy in copies[:4]:
+        copy.start()
+    total_ref[...] = jnp.sum(partials_ref[...], axis=0)
+    copies[4].start()
+    for copy in copies:
+        copy.wait()
+
+
 def by_rows(pair):
     return pair.reshape(2, ROWS, LANES).transpose(1, 0, 2).reshape(2 * ROWS, LANES)
 
@@ -226,7 +238,7 @@
         name="block_convolutions",
     )(blocks, *jax.tree.map(jnp.asarray, make_block_tables()))
     spectra = lax.all_to_all(sent, "ctx", 0, 0, tiled=True, axis_index_groups=HALF_ORDER)
-    like = jax.ShapeDtypeStruct(gate_q.shape, jnp.bfloat16)
+    like = pltpu.VMEM(gate_q.shape, jnp.bfloat16)
     *gated, partial_filter = pl.pallas_call(
         inverse_kernel,
         out_shape=(like, like, like, like, jax.ShapeDtypeStruct((groups, ROWS, LANES), f32)),
@@ -235,7 +247,15 @@
         name="inverse_transform",
     )(spectra, gate_q, gate_k, values, cotangent, skip_gain, *last, twiddle, *second_back)
     partials = lax.all_to_all(partial_filter, "chan", 0, 0, tiled=True, axis_index_groups=CHAN_ORDER)
-    grad_filter = jnp.sum(partials, axis=0)
+    like = jax.ShapeDtypeStruct(gate_q.shape, jnp.bfloat16)
+    *gated, grad_filter = pl.pallas_call(
+        finish_kernel,
+        out_shape=(like, like, like, like, jax.ShapeDtypeStruct((ROWS, LANES), f32)),
+        out_specs=[pl.BlockSpec(memory_space=pltpu.HBM)] * 5,
+        scratch_shapes=[pltpu.VMEM((ROWS, LANES), f32), pltpu.SemaphoreType.DMA((5,))],
+        compiler_params=SMALL,
+        name="finish",
+    )(partials, *gated)
     return (*map(by_channel, gated), grad_filter.reshape(BLOCK))
 
 

time: 60.6 us -> 59.9 us (0.988)
  other arithmetic: 0.62 us -> 0 us
    pallas_call x0 -> x1, Pallas kernels: none -> 0.67 us  [per_device(): pl.pallas_call(finish_kernel, out_shape=(like, like, like, like, jax.Shap...]
    pallas_call x1, Pallas kernels: 1.64 us -> 1.01 us  [per_device(): pl.pallas_call(inverse_kernel, out_shape=(like, like, like, like, jax.Sha...]
    reduce_sum x1 -> x0, other arithmetic: 0.62 us -> none  [per_device(): grad_filter = jnp.sum(partials, axis=0)]
where the time goes in v6:
time: 59.9 us; the launch traced here: 59.6 us
  blocking collectives  54.7 us (91%)
  Pallas kernels  3.88 us (6%)
  between operations  0.87 us (1%)
    all_to_all x1, blocking collectives, per_device(): lax.all_to_all(sent, 'ctx', 0, 0, tiled=True, axis_index_groups=CTX_ORDER)  31 us
    all_to_all x1, blocking collectives, per_device(): lax.all_to_all(sent, 'ctx', 0, 0, tiled=True, axis_index_groups=HALF_ORDER)  14.1 us
    all_to_all x1, blocking collectives, per_device(): lax.all_to_all(partial_filter, 'chan', 0, 0, tiled=True, axis_index_group...  9.7 us
    pallas_call x1, Pallas kernels, per_device(): pl.pallas_call(forward_kernel, out_shape=jax.ShapeDtypeStruct((BLOCKS, 1,...  1.51 us

profile of v6, /device:TPU:1, one launch (start us, length us, event | category | flops | bytes accessed | tf_op | source)
XLA Modules:
  0.0 59.6 jit_solution(3092112321939829161)
XLA Ops:
  0.6 1.5 %forward_transform.1 = f32[64,1,1280]{2,1,0:T(1,128)S(1)} custom-call(bf16[64,128]{1,0:T(8,128)(2,1)} %bitcast.42, bf16[64,128]{1,0:T(8,128)(2,1)} %bitcast.44, bf16[64,128]{1,0:T(8,128)(2,1)} %bitcast.46, bf16[64,128]{1,0:T(8,128)(2,1)} %bitcast.48, f32[32,128]{1,0:T(8,128)} %bitcast.50, bf16[128,192]{1,0:T(8,128)(2,1)} %constant.30.clone.refs_5_, ...), custom_call_target="tpu_custom_call" | custom-call | tf_op jit(solution)/shard_map/forward_transform/pallas_call | solution.py:222
  2.1 0.0 copy-start
  2.2 0.0 copy-start.1
  2.2 0.0 copy-start.10
  2.2 0.0 copy-start.11
  2.2 0.0 copy-start.12
  2.2 0.0 copy-start.13
  2.2 31.0 %all_to_all.15.in_ref = f32[64,1,1280]{2,1,0:T(1,128)S(1)} all-to-all(f32[64,1,1280]{2,1,0:T(1,128)S(1)} %forward_transform.1), channel_id=1, replica_groups={{416,264,272,280,288,296,304,312,320,328,336,344,352,360,368,376,384,39..., dimensions={0} | all-to-all | bytes 655360 | tf_op jit(solution)/shard_map/all_to_all | solution.py:233
  33.2 0.0 copy-done
  33.2 0.0 copy-done.1
  33.2 0.0 copy-done.10
  33.2 0.0 copy-done.11
  33.2 0.0 copy-done.12
  33.2 0.0 copy-done.13
  33.2 0.0 copy-start.7
  33.2 0.0 copy-start.8
  33.2 0.0 copy-start.9
  33.3 0.0 copy-start.14
  33.3 0.0 copy-start.15
  33.3 0.7 %block_convolutions.1 = f32[32,1,1280]{2,1,0:T(1,128)S(1)} custom-call(f32[64,1,1280]{2,1,0:T(1,128)S(1)} %all_to_all.15.in_ref, bf16[256,192]{1,0:T(8,128)(2,1)S(1)} %copy-done.1, bf16[256,192]{1,0:T(8,128)(2,1)S(1)} %copy-done, bf16[2,32,256]{2,1,0:T(8,128)(2,1)S(1)} %copy-done.13, bf16[2,32,256]{2,1,0:T(8,128)(2,1)S(1)} %copy-done.12, ...), custom_call_target="tpu_custom_call" | custom-call | tf_op jit(solution)/shard_map/block_convolutions/pallas_call | solution.py:234
  34.0 0.0 copy-start.2
  34.0 0.0 copy-start.3
  34.0 0.0 copy-start.4
  34.0 0.0 copy-start.5
  34.0 0.0 copy-start.6
  34.0 14.1 %all_to_all.16.in_ref = f32[32,1,1280]{2,1,0:T(1,128)S(1)} all-to-all(f32[32,1,1280]{2,1,0:T(1,128)S(1)} %block_convolutions.1), channel_id=1, replica_groups={{160,8,16,24,32,40,48,56,64,72,80,88,96,104,112,120,128,136,144,152,0,1..., dimensions={0} | all-to-all | bytes 327680 | tf_op jit(solution)/shard_map/all_to_all | solution.py:240
  48.1 0.0 copy-done.7
  48.1 0.0 copy-done.8
  48.1 0.0 copy-done.9
  48.1 0.0 copy-done.14
  48.1 0.0 copy-done.15
  48.1 0.0 copy-done.2
  48.1 0.0 copy-done.3
  48.2 0.0 copy-done.4
  48.2 0.0 copy-done.5
  48.2 0.0 copy-done.6
  48.2 1.0 %inverse_transform.1 = (bf16[64,128]{1,0:T(8,128)(2,1)S(1)}, bf16[64,128]{1,0:T(8,128)(2,1)S(1)}, bf16[64,128]{1,0:T(8,128)(2,1)S(1)}, bf16[64,128]{1,0:T(8,128)(2,1)S(1)}, f32[8,32,128]{2,1,0:T(8,128)S(1)}) custom-call(f32[32,1,1280]{2,1,0:T(1,128)S(1)} %all_to_all.16.in_ref, bf16[64,128]{1,0:T(8,128)(2,1)S(1)} %bitcast.49, bf16[64,128]{1,0:T(8,128)(2,1)S(1)} %bitcast.43, ...), custom_call_target="tpu_custom_call" | custom-call | tf_op jit(solution)/shard_map/inverse_transform/pallas_call | solution.py:242
  49.2 9.7 %all_to_all.17.partials_ref = f32[8,32,128]{2,1,0:T(8,128)S(1)} all-to-all(f32[8,32,128]{2,1,0:T(8,128)S(1)} %get-tuple-element.15), channel_id=1, replica_groups={{5,4,2,3,6,7,0,1},{13,12,10,11,14,15,8,9},{21,20,18,19,22,23,16,17},{29..., dimensions={0} | all-to-all | bytes 262144 | tf_op jit(solution)/shard_map/all_to_all | solution.py:249
  58.9 0.7 %finish.1 = (bf16[64,128]{1,0:T(8,128)(2,1)}, bf16[64,128]{1,0:T(8,128)(2,1)}, bf16[64,128]{1,0:T(8,128)(2,1)}, bf16[64,128]{1,0:T(8,128)(2,1)}, f32[32,128]{1,0:T(8,128)}) custom-call(f32[8,32,128]{2,1,0:T(8,128)S(1)} %all_to_all.17.partials_ref, bf16[64,128]{1,0:T(8,128)(2,1)S(1)} %get-tuple-element.16.refs_0_, ...), custom_call_target="tpu_custom_call" | custom-call | tf_op jit(solution)/shard_map/finish/pallas_call | solution.py:251
Async XLA Ops:
  2.1 31.0 %copy-start = (bf16[256,192]{1,0:T(8,128)(2,1)S(1)}, bf16[256,192]{1,0:T(8,128)(2,1)}, u32[]{:S(2)}) copy-start(bf16[256,192]{1,0:T(8,128)(2,1)} %constant.40.clone.filter_there_ref) | copy-start | bytes 294916
  2.2 31.0 %copy-start.1 = (bf16[256,192]{1,0:T(8,128)(2,1)S(1)}, bf16[256,192]{1,0:T(8,128)(2,1)}, u32[]{:S(2)}) copy-start(bf16[256,192]{1,0:T(8,128)(2,1)} %constant.39.clone.there_ref) | copy-start | bytes 294916
  2.2 31.0 %copy-start.10 = (bf16[2,32,256]{2,1,0:T(8,128)(2,1)S(1)}, bf16[2,32,256]{2,1,0:T(8,128)(2,1)}, u32[]{:S(2)}) copy-start(bf16[2,32,256]{2,1,0:T(8,128)(2,1)} %constant.44.clone.filter_low_ref) | copy-start | bytes 98308
  2.2 31.0 %copy-start.11 = (bf16[2,32,256]{2,1,0:T(8,128)(2,1)S(1)}, bf16[2,32,256]{2,1,0:T(8,128)(2,1)}, u32[]{:S(2)}) copy-start(bf16[2,32,256]{2,1,0:T(8,128)(2,1)} %constant.43.clone.filter_high_ref) | copy-start | bytes 98308
  2.2 31.0 %copy-start.12 = (bf16[2,32,256]{2,1,0:T(8,128)(2,1)S(1)}, bf16[2,32,256]{2,1,0:T(8,128)(2,1)}, u32[]{:S(2)}) copy-start(bf16[2,32,256]{2,1,0:T(8,128)(2,1)} %constant.42.clone.low_ref) | copy-start | bytes 98308
  2.2 31.0 %copy-start.13 = (bf16[2,32,256]{2,1,0:T(8,128)(2,1)S(1)}, bf16[2,32,256]{2,1,0:T(8,128)(2,1)}, u32[]{:S(2)}) copy-start(bf16[2,32,256]{2,1,0:T(8,128)(2,1)} %constant.41.clone.high_ref) | copy-start | bytes 98308
  33.2 14.9 %copy-start.7 = (bf16[2,4096]{1,0:T(2,128)(2,1)S(1)}, bf16[2,4096]{1,0:T(2,128)(2,1)}, u32[]{:S(2)}) copy-start(bf16[2,4096]{1,0:T(2,128)(2,1)} %param.26) | copy-start | bytes 49156
  33.2 14.9 %copy-start.8 = (bf16[2,4096]{1,0:T(2,128)(2,1)S(1)}, bf16[2,4096]{1,0:T(2,128)(2,1)}, u32[]{:S(2)}) copy-start(bf16[2,4096]{1,0:T(2,128)(2,1)} %param.21) | copy-start | bytes 49156
  33.2 14.9 %copy-start.9 = (bf16[64,384]{1,0:T(8,128)(2,1)S(1)}, bf16[64,384]{1,0:T(8,128)(2,1)}, u32[]{:S(2)}) copy-start(bf16[64,384]{1,0:T(8,128)(2,1)} %constant.32.clone.pair_ref) | copy-start | bytes 147460
  33.3 14.9 %copy-start.14 = (bf16[32,192]{1,0:T(8,128)(2,1)S(1)}, bf16[32,192]{1,0:T(8,128)(2,1)}, u32[]{:S(2)}) copy-start(bf16[32,192]{1,0:T(8,128)(2,1)} %constant.33.clone.last_ref) | copy-start | bytes 36868
  33.3 14.9 %copy-start.15 = (f32[2]{0:T(128)S(1)}, f32[2]{0:T(128)}, u32[]{:S(2)}) copy-start(f32[2]{0:T(128)} %gain_ref.1) | copy-start | bytes 28
  34.0 14.2 %copy-start.2 = (bf16[256,256]{1,0:T(8,128)(2,1)S(1)}, bf16[256,256]{1,0:T(8,128)(2,1)}, u32[]{:S(2)}) copy-start(bf16[256,256]{1,0:T(8,128)(2,1)} %constant.38.clone.low_ref) | copy-start | bytes 393220
  34.0 14.2 %copy-start.3 = (bf16[256,256]{1,0:T(8,128)(2,1)S(1)}, bf16[256,256]{1,0:T(8,128)(2,1)}, u32[]{:S(2)}) copy-start(bf16[256,256]{1,0:T(8,128)(2,1)} %constant.37.clone.high_ref) | copy-start | bytes 393220
  34.0 14.1 %copy-start.4 = (f32[2,32,128]{2,1,0:T(8,128)S(1)}, f32[2,32,128]{2,1,0:T(8,128)}, u32[]{:S(2)}) copy-start(f32[2,32,128]{2,1,0:T(8,128)} %constant.34.clone.refs_7_.twiddle_ref) | copy-start | bytes 98308
  34.0 14.1 %copy-start.5 = (bf16[2,4096]{1,0:T(2,128)(2,1)S(1)}, bf16[2,4096]{1,0:T(2,128)(2,1)}, u32[]{:S(2)}) copy-start(bf16[2,4096]{1,0:T(2,128)(2,1)} %param.22) | copy-start | bytes 49156
  34.0 14.1 %copy-start.6 = (bf16[2,4096]{1,0:T(2,128)(2,1)S(1)}, bf16[2,4096]{1,0:T(2,128)(2,1)}, u32[]{:S(2)}) copy-start(bf16[2,4096]{1,0:T(2,128)(2,1)} %param.23) | copy-start | bytes 49156

commit v7 on v6

--- a/solution.py
+++ b/solution.py
@@ -97,11 +97,11 @@
 
 
 def forward_kernel(*refs):
-    operands, (out_ref, *held, sems) = refs[:10], refs[10:]
+    operands, (out_ref, gain_ref, *held, sems) = refs[:11], refs[11:]
     copies = [pltpu.make_async_copy(src, dst, sems.at[n]) for n, (src, dst) in enumerate(zip(operands, held))]
     for copy in copies:
         copy.start()
-    key_ref, values_ref, cot_ref, query_ref, taps_ref, pair_ref, first_ref, twiddle_ref, high_ref, low_ref = held
+    key_ref, values_ref, cot_ref, query_ref, taps_ref, pair_ref, first_ref, twiddle_ref, high_ref, low_ref, skip_ref = held
     f32 = jnp.float32
     for copy in copies[:5]:
         copy.wait()
@@ -126,6 +126,8 @@
     for s in range(SIGNALS):
         for h in range(2):
             out_ref[HALVES * h : HALVES * (h + 1), 0, PAIR * s : PAIR * (s + 1)] = spectra[ROWS * s : ROWS * (s + 1)]
+    first_channel = lax.broadcasted_iota(jnp.int32, gain_ref.shape, 0) % 2 == 0
+    gain_ref[...] = jnp.where(first_channel, skip_ref[:, 0:1], skip_ref[:, 1:2])
 
 
 def blocks_kernel(in_ref, there_ref, filter_there_ref, high_ref, low_ref, filter_high_ref, filter_low_ref, out_ref):
@@ -183,8 +185,7 @@
     pairs = dot(pair_ref[...], stack3(pairs))
     query, cot = query_ref[...].astype(f32), cot_ref[...].astype(f32)
     key, value = key_ref[...].astype(f32), values_ref[...].astype(f32)
-    first_channel = lax.broadcasted_iota(jnp.int32, query.shape, 0) % 2 == 0
-    gain = jnp.where(first_channel, gain_ref[0], gain_ref[1])
+    gain = gain_ref[...]
     summed = pairs[:, :LANES] + gain * (key * value)
     out_ref[...] = (query * summed).astype(bf16)
     grad_query_ref[...] = (cot * summed).astype(bf16)
@@ -217,11 +218,10 @@
     first, last, twiddle, second, second_back = jax.tree.map(jnp.asarray, make_tables())
     groups = lax.axis_size("chan")
     gate_q, gate_k, values, cotangent = map(by_rows, (gate_q, gate_k, values, cotangent))
-    vmem = pl.BlockSpec(memory_space=pltpu.VMEM)
-    operands = (gate_k, values, cotangent, gate_q, filter_taps.reshape(ROWS, LANES), *first, twiddle, *second)
-    sent = pl.pallas_call(
+    operands = (gate_k, values, cotangent, gate_q, filter_taps.reshape(ROWS, LANES), *first, twiddle, *second, skip_gain[None])
+    sent, gain = pl.pallas_call(
         forward_kernel,
-        out_shape=jax.ShapeDtypeStruct((BLOCKS, 1, WIDTH), f32),
+        out_shape=(jax.ShapeDtypeStruct((BLOCKS, 1, WIDTH), f32), pltpu.VMEM(gate_q.shape, f32)),
         in_specs=[pl.BlockSpec(memory_space=pltpu.HBM)] * len(operands),
         scratch_shapes=[
             *(pltpu.VMEM(v.shape, v.dtype) for v in operands),
@@ -242,10 +242,9 @@
     *gated, partial_filter = pl.pallas_call(
         inverse_kernel,
         out_shape=(like, like, like, like, jax.ShapeDtypeStruct((groups, ROWS, LANES), f32)),
-        in_specs=[vmem] * 5 + [pl.BlockSpec(memory_space=pltpu.SMEM)] + [vmem] * 5,
         compiler_params=SMALL,
         name="inverse_transform",
-    )(spectra, gate_q, gate_k, values, cotangent, skip_gain, *last, twiddle, *second_back)
+    )(spectra, gate_q, gate_k, values, cotangent, gain, *last, twiddle, *second_back)
     partials = lax.all_to_all(partial_filter, "chan", 0, 0, tiled=True, axis_index_groups=CHAN_ORDER)
     like = jax.ShapeDtypeStruct(gate_q.shape, jnp.bfloat16)
     *gated, grad_filter = pl.pallas_call(

time: 59.9 us -> 59.3 us (0.990)
  no operation moved by 1% of the time
where the time goes in v7:
time: 59.3 us; the launch traced here: 59 us
  blocking collectives  54.7 us (92%)
  Pallas kernels  3.36 us (6%)
  between operations  0.85 us (1%)
    all_to_all x1, blocking collectives, per_device(): lax.all_to_all(sent, 'ctx', 0, 0, tiled=True, axis_index_groups=CTX_ORDER)  31 us
    all_to_all x1, blocking collectives, per_device(): lax.all_to_all(sent, 'ctx', 0, 0, tiled=True, axis_index_groups=HALF_ORDER)  13.8 us
    all_to_all x1, blocking collectives, per_device(): lax.all_to_all(partial_filter, 'chan', 0, 0, tiled=True, axis_index_group...  9.91 us
    pallas_call x1, Pallas kernels, per_device(): pl.pallas_call(forward_kernel, out_shape=(jax.ShapeDtypeStruct((BLOCKS, 1...  1.52 us

profile of v7, /device:TPU:1, one launch (start us, length us, event | category | flops | bytes accessed | tf_op | source)
XLA Modules:
  0.0 59.0 jit_solution(13177748221173699564)
XLA Ops:
  0.6 1.5 %forward_transform.1 = (f32[64,1,1280]{2,1,0:T(1,128)S(1)}, f32[64,128]{1,0:T(8,128)S(1)}) custom-call(bf16[64,128]{1,0:T(8,128)(2,1)} %bitcast.43, bf16[64,128]{1,0:T(8,128)(2,1)} %bitcast.45, bf16[64,128]{1,0:T(8,128)(2,1)} %bitcast.47, bf16[64,128]{1,0:T(8,128)(2,1)} %bitcast.49, f32[32,128]{1,0:T(8,128)} %bitcast.51, ...), custom_call_target="tpu_custom_call" | custom-call | tf_op jit(solution)/shard_map/forward_transform/pallas_call | solution.py:222
  2.2 0.0 copy-start.2
  2.2 0.0 copy-start.3
  2.2 0.0 copy-start.10
  2.2 0.0 copy-start.11
  2.2 0.0 copy-start.12
  2.2 0.0 copy-start.13
  2.2 31.0 %all_to_all.15.in_ref = f32[64,1,1280]{2,1,0:T(1,128)S(1)} all-to-all(f32[64,1,1280]{2,1,0:T(1,128)S(1)} %get-tuple-element.17), channel_id=1, replica_groups={{416,264,272,280,288,296,304,312,320,328,336,344,352,360,368,376,384,39..., dimensions={0} | all-to-all | bytes 655360 | tf_op jit(solution)/shard_map/all_to_all | solution.py:233
  33.2 0.0 copy-done.2
  33.2 0.0 copy-done.3
  33.2 0.0 copy-done.10
  33.2 0.0 copy-done.11
  33.2 0.0 copy-done.12
  33.2 0.0 copy-done.13
  33.2 0.0 copy-start.7
  33.2 0.0 copy-start.8
  33.3 0.0 copy-start.9
  33.3 0.0 copy-start.14
  33.3 0.7 %block_convolutions.1 = f32[32,1,1280]{2,1,0:T(1,128)S(1)} custom-call(f32[64,1,1280]{2,1,0:T(1,128)S(1)} %all_to_all.15.in_ref, bf16[256,192]{1,0:T(8,128)(2,1)S(1)} %copy-done.3, bf16[256,192]{1,0:T(8,128)(2,1)S(1)} %copy-done.2, bf16[2,32,256]{2,1,0:T(8,128)(2,1)S(1)} %copy-done.13, bf16[2,32,256]{2,1,0:T(8,128)(2,1)S(1)} %copy-done.12, ...), custom_call_target="tpu_custom_call" | custom-call | tf_op jit(solution)/shard_map/block_convolutions/pallas_call | solution.py:234
  34.0 0.0 copy-start
  34.0 0.0 copy-start.1
  34.0 0.0 copy-start.4
  34.0 0.0 copy-start.5
  34.0 0.0 copy-start.6
  34.0 13.8 %all_to_all.16.in_ref = f32[32,1,1280]{2,1,0:T(1,128)S(1)} all-to-all(f32[32,1,1280]{2,1,0:T(1,128)S(1)} %block_convolutions.1), channel_id=1, replica_groups={{160,8,16,24,32,40,48,56,64,72,80,88,96,104,112,120,128,136,144,152,0,1..., dimensions={0} | all-to-all | bytes 327680 | tf_op jit(solution)/shard_map/all_to_all | solution.py:240
  47.9 0.0 copy-done.7
  47.9 0.0 copy-done.8
  47.9 0.0 copy-done.9
  47.9 0.0 copy-done.14
  47.9 0.0 copy-done
  47.9 0.0 copy-done.1
  47.9 0.0 copy-done.4
  47.9 0.0 copy-done.5
  48.0 0.0 copy-done.6
  48.0 0.5 inverse_transform.1
  48.4 9.9 %all_to_all.17.partials_ref = f32[8,32,128]{2,1,0:T(8,128)S(1)} all-to-all(f32[8,32,128]{2,1,0:T(8,128)S(1)} %get-tuple-element.19), channel_id=1, replica_groups={{5,4,2,3,6,7,0,1},{13,12,10,11,14,15,8,9},{21,20,18,19,22,23,16,17},{29..., dimensions={0} | all-to-all | bytes 262144 | tf_op jit(solution)/shard_map/all_to_all | solution.py:248
  58.4 0.7 %finish.1 = (bf16[64,128]{1,0:T(8,128)(2,1)}, bf16[64,128]{1,0:T(8,128)(2,1)}, bf16[64,128]{1,0:T(8,128)(2,1)}, bf16[64,128]{1,0:T(8,128)(2,1)}, f32[32,128]{1,0:T(8,128)}) custom-call(f32[8,32,128]{2,1,0:T(8,128)S(1)} %all_to_all.17.partials_ref, bf16[64,128]{1,0:T(8,128)(2,1)S(1)} %get-tuple-element.20.refs_0_, ...), custom_call_target="tpu_custom_call" | custom-call | tf_op jit(solution)/shard_map/finish/pallas_call | solution.py:250
Async XLA Ops:
  2.2 31.0 %copy-start.2 = (bf16[256,192]{1,0:T(8,128)(2,1)S(1)}, bf16[256,192]{1,0:T(8,128)(2,1)}, u32[]{:S(2)}) copy-start(bf16[256,192]{1,0:T(8,128)(2,1)} %constant.40.clone.filter_there_ref) | copy-start | bytes 294916
  2.2 31.0 %copy-start.3 = (bf16[256,192]{1,0:T(8,128)(2,1)S(1)}, bf16[256,192]{1,0:T(8,128)(2,1)}, u32[]{:S(2)}) copy-start(bf16[256,192]{1,0:T(8,128)(2,1)} %constant.39.clone.there_ref) | copy-start | bytes 294916
  2.2 31.0 %copy-start.10 = (bf16[2,32,256]{2,1,0:T(8,128)(2,1)S(1)}, bf16[2,32,256]{2,1,0:T(8,128)(2,1)}, u32[]{:S(2)}) copy-start(bf16[2,32,256]{2,1,0:T(8,128)(2,1)} %constant.44.clone.filter_low_ref) | copy-start | bytes 98308
  2.2 31.0 %copy-start.11 = (bf16[2,32,256]{2,1,0:T(8,128)(2,1)S(1)}, bf16[2,32,256]{2,1,0:T(8,128)(2,1)}, u32[]{:S(2)}) copy-start(bf16[2,32,256]{2,1,0:T(8,128)(2,1)} %constant.43.clone.filter_high_ref) | copy-start | bytes 98308
  2.2 31.0 %copy-start.12 = (bf16[2,32,256]{2,1,0:T(8,128)(2,1)S(1)}, bf16[2,32,256]{2,1,0:T(8,128)(2,1)}, u32[]{:S(2)}) copy-start(bf16[2,32,256]{2,1,0:T(8,128)(2,1)} %constant.42.clone.low_ref) | copy-start | bytes 98308
  2.2 31.0 %copy-start.13 = (bf16[2,32,256]{2,1,0:T(8,128)(2,1)S(1)}, bf16[2,32,256]{2,1,0:T(8,128)(2,1)}, u32[]{:S(2)}) copy-start(bf16[2,32,256]{2,1,0:T(8,128)(2,1)} %constant.41.clone.high_ref) | copy-start | bytes 98308
  33.2 14.7 %copy-start.7 = (bf16[2,4096]{1,0:T(2,128)(2,1)S(1)}, bf16[2,4096]{1,0:T(2,128)(2,1)}, u32[]{:S(2)}) copy-start(bf16[2,4096]{1,0:T(2,128)(2,1)} %param.26) | copy-start | bytes 49156
  33.2 14.7 %copy-start.8 = (bf16[2,4096]{1,0:T(2,128)(2,1)S(1)}, bf16[2,4096]{1,0:T(2,128)(2,1)}, u32[]{:S(2)}) copy-start(bf16[2,4096]{1,0:T(2,128)(2,1)} %param.21) | copy-start | bytes 49156
  33.3 14.6 %copy-start.9 = (bf16[64,384]{1,0:T(8,128)(2,1)S(1)}, bf16[64,384]{1,0:T(8,128)(2,1)}, u32[]{:S(2)}) copy-start(bf16[64,384]{1,0:T(8,128)(2,1)} %constant.32.clone.pair_ref) | copy-start | bytes 147460
  33.3 14.6 %copy-start.14 = (bf16[32,192]{1,0:T(8,128)(2,1)S(1)}, bf16[32,192]{1,0:T(8,128)(2,1)}, u32[]{:S(2)}) copy-start(bf16[32,192]{1,0:T(8,128)(2,1)} %constant.33.clone.last_ref) | copy-start | bytes 36868
  34.0 13.9 %copy-start = (bf16[256,256]{1,0:T(8,128)(2,1)S(1)}, bf16[256,256]{1,0:T(8,128)(2,1)}, u32[]{:S(2)}) copy-start(bf16[256,256]{1,0:T(8,128)(2,1)} %constant.38.clone.low_ref) | copy-start | bytes 393220
  34.0 13.9 %copy-start.1 = (bf16[256,256]{1,0:T(8,128)(2,1)S(1)}, bf16[256,256]{1,0:T(8,128)(2,1)}, u32[]{:S(2)}) copy-start(bf16[256,256]{1,0:T(8,128)(2,1)} %constant.37.clone.high_ref) | copy-start | bytes 393220
  34.0 13.9 %copy-start.4 = (f32[2,32,128]{2,1,0:T(8,128)S(1)}, f32[2,32,128]{2,1,0:T(8,128)}, u32[]{:S(2)}) copy-start(f32[2,32,128]{2,1,0:T(8,128)} %constant.34.clone.refs_7_.twiddle_ref) | copy-start | bytes 98308
  34.0 13.9 %copy-start.5 = (bf16[2,4096]{1,0:T(2,128)(2,1)S(1)}, bf16[2,4096]{1,0:T(2,128)(2,1)}, u32[]{:S(2)}) copy-start(bf16[2,4096]{1,0:T(2,128)(2,1)} %param.22) | copy-start | bytes 49156
  34.0 13.9 %copy-start.6 = (bf16[2,4096]{1,0:T(2,128)(2,1)S(1)}, bf16[2,4096]{1,0:T(2,128)(2,1)}, u32[]{:S(2)}) copy-start(bf16[2,4096]{1,0:T(2,128)(2,1)} %param.23) | copy-start | bytes 49156

commit v8 on v7

--- a/solution.py
+++ b/solution.py
@@ -16,10 +16,13 @@
 PAIR = 2 * LANES
 WIDTH = SIGNALS * PAIR
 SMALL = pltpu.CompilerParams(vmem_limit_bytes=8 << 20)
-CORNER = 20
-PLANE_ORDER = [CORNER if p == 0 else 0 if p == CORNER else p for p in range(HALVES)]
-CTX_ORDER = [[HALVES + p for p in PLANE_ORDER] + PLANE_ORDER]
-HALF_ORDER = [PLANE_ORDER, [HALVES + p for p in PLANE_ORDER]]
+def plane_order(corner):
+    return [corner if p == 0 else 0 if p == corner else p for p in range(HALVES)]
+
+
+FIRST_ORDER, SECOND_ORDER = plane_order(21), plane_order(20)
+CTX_ORDER = [[HALVES + p for p in FIRST_ORDER] + FIRST_ORDER]
+HALF_ORDER = [SECOND_ORDER, [HALVES + p for p in SECOND_ORDER]]
 CHAN_ORDER = [[5, 4, 2, 3, 6, 7, 0, 1]]
 
 
@@ -41,7 +44,8 @@
     first = np.concatenate([first.real, first.imag], 0)
     first_pair = np.zeros((2, 2 * ROWS, ROWS, 2))
     first_pair[0, :, :, 0] = first_pair[1, :, :, 1] = first
-    last = np.exp(2j * np.pi * (a[:, None] * a[None, :] / ROWS + LANES * a[:, None] / (4 * BLOCK)))
+    k1 = np.array([FIRST_ORDER.index(p) for p in SECOND_ORDER])
+    last = np.exp(2j * np.pi * (a[:, None] * k1[None, :] / ROWS + LANES * a[:, None] / (4 * BLOCK)))
     last = np.concatenate([last.real, -last.imag], 1) / BLOCK / (BLOCK * BLOCKS) ** 0.5
     last_pair = np.zeros((ROWS, 2, 2, 2 * ROWS))
     last_pair[:, 0, 0] = last_pair[:, 1, 1] = last
@@ -54,6 +58,7 @@
     last_table = thrice(last_pair.reshape(2 * ROWS, 4 * ROWS)), thrice(last)
     twiddle = np.exp(-2j * np.pi * b[None, :] * (4 * a[:, None] + 1) / (4 * BLOCK))
     twiddle = np.stack([twiddle.real, twiddle.imag]).astype(np.float32)
+    twiddle = twiddle, twiddle[:, k1]
     angle = 2 * np.pi * (b[:, None] * b[None, :] % LANES) / LANES
     cos, sin = np.cos(angle), np.sin(angle)
     second = np.block([[cos, -sin], [sin, cos]])
@@ -62,21 +67,21 @@
 
 def make_block_tables():
     blocks = np.array(CTX_ORDER[0])
+    results = np.array(HALF_ORDER)
     phases = np.arange(2 * BLOCKS)
     wave = np.exp(-2j * np.pi * phases[:, None] * blocks[None, :] / (2 * BLOCKS))
     step = np.exp(-2j * np.pi * phases / (2 * BLOCKS))
-    back = np.conj(wave.T) / (2 * BLOCKS)
+    back = np.exp(2j * np.pi * results[:, :, None] * phases / (2 * BLOCKS)) / (2 * BLOCKS)
 
     def there(table):
         high, low = split_table(np.concatenate([table.real, -table.imag], 0))
         return np.concatenate([high, low, high], 1)
 
     def here(table):
-        rows = [table[HALVES:], table[:HALVES]]
-        return split_table(np.stack([np.concatenate([t.real, t.imag], 1) for t in rows]))
+        return split_table(np.concatenate([table.real, table.imag], 2))
 
     filter_wave = wave * (1 + 1j * step)[:, None]
-    filter_back = back * (1 - 1j * np.conj(step))[None, :]
+    filter_back = back * (1 - 1j * np.conj(step))
     return there(wave), there(filter_wave), *here(back), *here(filter_back)
 
 
@@ -218,7 +223,7 @@
     first, last, twiddle, second, second_back = jax.tree.map(jnp.asarray, make_tables())
     groups = lax.axis_size("chan")
     gate_q, gate_k, values, cotangent = map(by_rows, (gate_q, gate_k, values, cotangent))
-    operands = (gate_k, values, cotangent, gate_q, filter_taps.reshape(ROWS, LANES), *first, twiddle, *second, skip_gain[None])
+    operands = (gate_k, values, cotangent, gate_q, filter_taps.reshape(ROWS, LANES), *first, twiddle[0], *second, skip_gain[None])
     sent, gain = pl.pallas_call(
         forward_kernel,
         out_shape=(jax.ShapeDtypeStruct((BLOCKS, 1, WIDTH), f32), pltpu.VMEM(gate_q.shape, f32)),
@@ -244,7 +249,7 @@
         out_shape=(like, like, like, like, jax.ShapeDtypeStruct((groups, ROWS, LANES), f32)),
         compiler_params=SMALL,
         name="inverse_transform",
-    )(spectra, gate_q, gate_k, values, cotangent, gain, *last, twiddle, *second_back)
+    )(spectra, gate_q, gate_k, values, cotangent, gain, *last, twiddle[1], *second_back)
     partials = lax.all_to_all(partial_filter, "chan", 0, 0, tiled=True, axis_index_groups=CHAN_ORDER)
     like = jax.ShapeDtypeStruct(gate_q.shape, jnp.bfloat16)
     *gated, grad_filter = pl.pallas_call(

time: 59.3 us -> 58.1 us (0.980)
  blocking collectives: 54.7 us -> 53.5 us
    all_to_all x1, blocking collectives: 13.8 us -> 12.6 us  [per_device(): lax.all_to_all(sent, 'ctx', 0, 0, tiled=True, axis_index_groups=HALF_ORDER)]
where the time goes in v8:
time: 58.1 us; the launch traced here: 57.8 us
  blocking collectives  53.5 us (92%)
  Pallas kernels  3.36 us (6%)
  between operations  0.85 us (1%)
    all_to_all x1, blocking collectives, per_device(): lax.all_to_all(sent, 'ctx', 0, 0, tiled=True, axis_index_groups=CTX_ORDER)  30.8 us
    all_to_all x1, blocking collectives, per_device(): lax.all_to_all(sent, 'ctx', 0, 0, tiled=True, axis_index_groups=HALF_ORDER)  12.6 us
    all_to_all x1, blocking collectives, per_device(): lax.all_to_all(partial_filter, 'chan', 0, 0, tiled=True, axis_index_group...  10.1 us
    pallas_call x1, Pallas kernels, per_device(): pl.pallas_call(forward_kernel, out_shape=(jax.ShapeDtypeStruct((BLOCKS, 1...  1.52 us

profile of v8, /device:TPU:1, one launch (start us, length us, event | category | flops | bytes accessed | tf_op | source)
XLA Modules:
  0.0 57.8 jit_solution(17888246484006133442)
XLA Ops:
  0.6 1.5 %forward_transform.1 = (f32[64,1,1280]{2,1,0:T(1,128)S(1)}, f32[64,128]{1,0:T(8,128)S(1)}) custom-call(bf16[64,128]{1,0:T(8,128)(2,1)} %bitcast.43, bf16[64,128]{1,0:T(8,128)(2,1)} %bitcast.45, bf16[64,128]{1,0:T(8,128)(2,1)} %bitcast.47, bf16[64,128]{1,0:T(8,128)(2,1)} %bitcast.49, f32[32,128]{1,0:T(8,128)} %bitcast.51, ...), custom_call_target="tpu_custom_call" | custom-call | tf_op jit(solution)/shard_map/forward_transform/pallas_call | solution.py:227
  2.2 0.0 copy-start.2
  2.2 0.0 copy-start.3
  2.2 0.0 copy-start.9
  2.2 0.0 copy-start.10
  2.2 0.0 copy-start.11
  2.2 0.0 copy-start.12
  2.2 30.8 %all_to_all.15.in_ref = f32[64,1,1280]{2,1,0:T(1,128)S(1)} all-to-all(f32[64,1,1280]{2,1,0:T(1,128)S(1)} %get-tuple-element.17), channel_id=1, replica_groups={{424,264,272,280,288,296,304,312,320,328,336,344,352,360,368,376,384,39..., dimensions={0} | all-to-all | bytes 655360 | tf_op jit(solution)/shard_map/all_to_all | solution.py:238
  33.1 0.0 copy-done.2
  33.1 0.0 copy-done.3
  33.1 0.0 copy-done.9
  33.1 0.0 copy-done.10
  33.1 0.0 copy-done.11
  33.1 0.0 copy-done.12
  33.1 0.0 copy-start.8
  33.1 0.0 copy-start.13
  33.1 0.0 copy-start.14
  33.1 0.7 %block_convolutions.1 = f32[32,1,1280]{2,1,0:T(1,128)S(1)} custom-call(f32[64,1,1280]{2,1,0:T(1,128)S(1)} %all_to_all.15.in_ref, bf16[256,192]{1,0:T(8,128)(2,1)S(1)} %copy-done.3, bf16[256,192]{1,0:T(8,128)(2,1)S(1)} %copy-done.2, bf16[2,32,256]{2,1,0:T(8,128)(2,1)S(1)} %copy-done.12, bf16[2,32,256]{2,1,0:T(8,128)(2,1)S(1)} %copy-done.11, ...), custom_call_target="tpu_custom_call" | custom-call | tf_op jit(solution)/shard_map/block_convolutions/pallas_call | solution.py:239
  33.8 0.0 copy-start
  33.9 0.0 copy-start.1
  33.9 0.0 copy-start.4
  33.9 0.0 copy-start.5
  33.9 0.0 copy-start.6
  33.9 0.0 copy-start.7
  33.9 12.6 %all_to_all.16.in_ref = f32[32,1,1280]{2,1,0:T(1,128)S(1)} all-to-all(f32[32,1,1280]{2,1,0:T(1,128)S(1)} %block_convolutions.1), channel_id=1, replica_groups={{160,8,16,24,32,40,48,56,64,72,80,88,96,104,112,120,128,136,144,152,0,1..., dimensions={0} | all-to-all | bytes 327680 | tf_op jit(solution)/shard_map/all_to_all | solution.py:245
  46.5 0.0 copy-done.8
  46.5 0.0 copy-done.13
  46.5 0.0 copy-done.14
  46.5 0.0 copy-done
  46.5 0.0 copy-done.1
  46.5 0.0 copy-done.4
  46.6 0.0 copy-done.5
  46.6 0.0 copy-done.6
  46.6 0.0 copy-done.7
  46.6 0.5 inverse_transform.1
  47.1 10.1 %all_to_all.17.partials_ref = f32[8,32,128]{2,1,0:T(8,128)S(1)} all-to-all(f32[8,32,128]{2,1,0:T(8,128)S(1)} %get-tuple-element.19), channel_id=1, replica_groups={{5,4,2,3,6,7,0,1},{13,12,10,11,14,15,8,9},{21,20,18,19,22,23,16,17},{29..., dimensions={0} | all-to-all | bytes 262144 | tf_op jit(solution)/shard_map/all_to_all | solution.py:253
  57.2 0.7 %finish.1 = (bf16[64,128]{1,0:T(8,128)(2,1)}, bf16[64,128]{1,0:T(8,128)(2,1)}, bf16[64,128]{1,0:T(8,128)(2,1)}, bf16[64,128]{1,0:T(8,128)(2,1)}, f32[32,128]{1,0:T(8,128)}) custom-call(f32[8,32,128]{2,1,0:T(8,128)S(1)} %all_to_all.17.partials_ref, bf16[64,128]{1,0:T(8,128)(2,1)S(1)} %get-tuple-element.20.refs_0_, ...), custom_call_target="tpu_custom_call" | custom-call | tf_op jit(solution)/shard_map/finish/pallas_call | solution.py:255
Async XLA Ops:
  2.2 30.9 %copy-start.2 = (bf16[256,192]{1,0:T(8,128)(2,1)S(1)}, bf16[256,192]{1,0:T(8,128)(2,1)}, u32[]{:S(2)}) copy-start(bf16[256,192]{1,0:T(8,128)(2,1)} %constant.43.clone.filter_there_ref) | copy-start | bytes 294916
  2.2 30.9 %copy-start.3 = (bf16[256,192]{1,0:T(8,128)(2,1)S(1)}, bf16[256,192]{1,0:T(8,128)(2,1)}, u32[]{:S(2)}) copy-start(bf16[256,192]{1,0:T(8,128)(2,1)} %constant.42.clone.there_ref) | copy-start | bytes 294916
  2.2 30.9 %copy-start.9 = (bf16[2,32,256]{2,1,0:T(8,128)(2,1)S(1)}, bf16[2,32,256]{2,1,0:T(8,128)(2,1)}, u32[]{:S(2)}) copy-start(bf16[2,32,256]{2,1,0:T(8,128)(2,1)} %constant.47.clone.filter_low_ref) | copy-start | bytes 98308
  2.2 30.9 %copy-start.10 = (bf16[2,32,256]{2,1,0:T(8,128)(2,1)S(1)}, bf16[2,32,256]{2,1,0:T(8,128)(2,1)}, u32[]{:S(2)}) copy-start(bf16[2,32,256]{2,1,0:T(8,128)(2,1)} %constant.46.clone.filter_high_ref) | copy-start | bytes 98308
  2.2 30.9 %copy-start.11 = (bf16[2,32,256]{2,1,0:T(8,128)(2,1)S(1)}, bf16[2,32,256]{2,1,0:T(8,128)(2,1)}, u32[]{:S(2)}) copy-start(bf16[2,32,256]{2,1,0:T(8,128)(2,1)} %constant.45.clone.low_ref) | copy-start | bytes 98308
  2.2 30.9 %copy-start.12 = (bf16[2,32,256]{2,1,0:T(8,128)(2,1)S(1)}, bf16[2,32,256]{2,1,0:T(8,128)(2,1)}, u32[]{:S(2)}) copy-start(bf16[2,32,256]{2,1,0:T(8,128)(2,1)} %constant.44.clone.high_ref) | copy-start | bytes 98308
  33.1 13.4 %copy-start.8 = (bf16[64,384]{1,0:T(8,128)(2,1)S(1)}, bf16[64,384]{1,0:T(8,128)(2,1)}, u32[]{:S(2)}) copy-start(bf16[64,384]{1,0:T(8,128)(2,1)} %constant.34.clone.pair_ref) | copy-start | bytes 147460
  33.1 13.4 %copy-start.13 = (f32[2,32,128]{2,1,0:T(8,128)S(1)}, f32[2,32,128]{2,1,0:T(8,128)}, u32[]{:S(2)}) copy-start(f32[2,32,128]{2,1,0:T(8,128)} %constant.37.clone.twiddle_ref) | copy-start | bytes 98308
  33.1 13.4 %copy-start.14 = (bf16[32,192]{1,0:T(8,128)(2,1)S(1)}, bf16[32,192]{1,0:T(8,128)(2,1)}, u32[]{:S(2)}) copy-start(bf16[32,192]{1,0:T(8,128)(2,1)} %constant.35.clone.last_ref) | copy-start | bytes 36868
  33.8 12.7 %copy-start = (bf16[256,256]{1,0:T(8,128)(2,1)S(1)}, bf16[256,256]{1,0:T(8,128)(2,1)}, u32[]{:S(2)}) copy-start(bf16[256,256]{1,0:T(8,128)(2,1)} %constant.41.clone.low_ref) | copy-start | bytes 393220
  33.9 12.7 %copy-start.1 = (bf16[256,256]{1,0:T(8,128)(2,1)S(1)}, bf16[256,256]{1,0:T(8,128)(2,1)}, u32[]{:S(2)}) copy-start(bf16[256,256]{1,0:T(8,128)(2,1)} %constant.40.clone.high_ref) | copy-start | bytes 393220
  33.9 12.7 %copy-start.4 = (bf16[2,4096]{1,0:T(2,128)(2,1)S(1)}, bf16[2,4096]{1,0:T(2,128)(2,1)}, u32[]{:S(2)}) copy-start(bf16[2,4096]{1,0:T(2,128)(2,1)} %param.23) | copy-start | bytes 49156
  33.9 12.7 %copy-start.5 = (bf16[2,4096]{1,0:T(2,128)(2,1)S(1)}, bf16[2,4096]{1,0:T(2,128)(2,1)}, u32[]{:S(2)}) copy-start(bf16[2,4096]{1,0:T(2,128)(2,1)} %param.24) | copy-start | bytes 49156
  33.9 12.7 %copy-start.6 = (bf16[2,4096]{1,0:T(2,128)(2,1)S(1)}, bf16[2,4096]{1,0:T(2,128)(2,1)}, u32[]{:S(2)}) copy-start(bf16[2,4096]{1,0:T(2,128)(2,1)} %param.27) | copy-start | bytes 49156
  33.9 12.7 %copy-start.7 = (bf16[2,4096]{1,0:T(2,128)(2,1)S(1)}, bf16[2,4096]{1,0:T(2,128)(2,1)}, u32[]{:S(2)}) copy-start(bf16[2,4096]{1,0:T(2,128)(2,1)} %param.22) | copy-start | bytes 49156

commit v9 on v8

--- a/solution.py
+++ b/solution.py
@@ -20,7 +20,7 @@
     return [corner if p == 0 else 0 if p == corner else p for p in range(HALVES)]
 
 
-FIRST_ORDER, SECOND_ORDER = plane_order(21), plane_order(20)
+FIRST_ORDER, SECOND_ORDER = plane_order(22), plane_order(20)
 CTX_ORDER = [[HALVES + p for p in FIRST_ORDER] + FIRST_ORDER]
 HALF_ORDER = [SECOND_ORDER, [HALVES + p for p in SECOND_ORDER]]
 CHAN_ORDER = [[5, 4, 2, 3, 6, 7, 0, 1]]

time: 58.1 us -> 58.1 us (level)
  no operation moved by 1% of the time
where the time goes in v9:
time: 58.1 us; the launch traced here: 57.8 us
  blocking collectives  53.5 us (92%)
  Pallas kernels  3.35 us (6%)
  between operations  0.85 us (1%)
    all_to_all x1, blocking collectives, per_device(): lax.all_to_all(sent, 'ctx', 0, 0, tiled=True, axis_index_groups=CTX_ORDER)  30.5 us
    all_to_all x1, blocking collectives, per_device(): lax.all_to_all(sent, 'ctx', 0, 0, tiled=True, axis_index_groups=HALF_ORDER)  12.8 us
    all_to_all x1, blocking collectives, per_device(): lax.all_to_all(partial_filter, 'chan', 0, 0, tiled=True, axis_index_group...  10.2 us
    pallas_call x1, Pallas kernels, per_device(): pl.pallas_call(forward_kernel, out_shape=(jax.ShapeDtypeStruct((BLOCKS, 1...  1.52 us

profile of v9, /device:TPU:1, one launch (start us, length us, event | category | flops | bytes accessed | tf_op | source)
XLA Modules:
  0.0 57.8 jit_solution(11107219047768598446)
XLA Ops:
  0.6 1.5 %forward_transform.1 = (f32[64,1,1280]{2,1,0:T(1,128)S(1)}, f32[64,128]{1,0:T(8,128)S(1)}) custom-call(bf16[64,128]{1,0:T(8,128)(2,1)} %bitcast.43, bf16[64,128]{1,0:T(8,128)(2,1)} %bitcast.45, bf16[64,128]{1,0:T(8,128)(2,1)} %bitcast.47, bf16[64,128]{1,0:T(8,128)(2,1)} %bitcast.49, f32[32,128]{1,0:T(8,128)} %bitcast.51, ...), custom_call_target="tpu_custom_call" | custom-call | tf_op jit(solution)/shard_map/forward_transform/pallas_call | solution.py:227
  2.2 0.0 copy-start.2
  2.2 0.0 copy-start.3
  2.2 0.0 copy-start.9
  2.2 0.0 copy-start.10
  2.2 0.0 copy-start.11
  2.2 0.0 copy-start.12
  2.2 30.5 %all_to_all.15.in_ref = f32[64,1,1280]{2,1,0:T(1,128)S(1)} all-to-all(f32[64,1,1280]{2,1,0:T(1,128)S(1)} %get-tuple-element.17), channel_id=1, replica_groups={{432,264,272,280,288,296,304,312,320,328,336,344,352,360,368,376,384,39..., dimensions={0} | all-to-all | bytes 655360 | tf_op jit(solution)/shard_map/all_to_all | solution.py:238
  32.8 0.0 copy-done.2
  32.8 0.0 copy-done.3
  32.8 0.0 copy-done.9
  32.8 0.0 copy-done.10
  32.8 0.0 copy-done.11
  32.8 0.0 copy-done.12
  32.8 0.0 copy-start.8
  32.8 0.0 copy-start.13
  32.8 0.0 copy-start.14
  32.8 0.7 %block_convolutions.1 = f32[32,1,1280]{2,1,0:T(1,128)S(1)} custom-call(f32[64,1,1280]{2,1,0:T(1,128)S(1)} %all_to_all.15.in_ref, bf16[256,192]{1,0:T(8,128)(2,1)S(1)} %copy-done.3, bf16[256,192]{1,0:T(8,128)(2,1)S(1)} %copy-done.2, bf16[2,32,256]{2,1,0:T(8,128)(2,1)S(1)} %copy-done.12, bf16[2,32,256]{2,1,0:T(8,128)(2,1)S(1)} %copy-done.11, ...), custom_call_target="tpu_custom_call" | custom-call | tf_op jit(solution)/shard_map/block_convolutions/pallas_call | solution.py:239
  33.5 0.0 copy-start
  33.6 0.0 copy-start.1
  33.6 0.0 copy-start.4
  33.6 0.0 copy-start.5
  33.6 0.0 copy-start.6
  33.6 0.0 copy-start.7
  33.6 12.8 %all_to_all.16.in_ref = f32[32,1,1280]{2,1,0:T(1,128)S(1)} all-to-all(f32[32,1,1280]{2,1,0:T(1,128)S(1)} %block_convolutions.1), channel_id=1, replica_groups={{160,8,16,24,32,40,48,56,64,72,80,88,96,104,112,120,128,136,144,152,0,1..., dimensions={0} | all-to-all | bytes 327680 | tf_op jit(solution)/shard_map/all_to_all | solution.py:245
  46.4 0.0 copy-done.8
  46.4 0.0 copy-done.13
  46.4 0.0 copy-done.14
  46.4 0.0 copy-done
  46.4 0.0 copy-done.1
  46.4 0.0 copy-done.4
  46.5 0.0 copy-done.5
  46.5 0.0 copy-done.6
  46.5 0.0 copy-done.7
  46.5 0.5 inverse_transform.1
  47.0 10.2 %all_to_all.17.partials_ref = f32[8,32,128]{2,1,0:T(8,128)S(1)} all-to-all(f32[8,32,128]{2,1,0:T(8,128)S(1)} %get-tuple-element.19), channel_id=1, replica_groups={{5,4,2,3,6,7,0,1},{13,12,10,11,14,15,8,9},{21,20,18,19,22,23,16,17},{29..., dimensions={0} | all-to-all | bytes 262144 | tf_op jit(solution)/shard_map/all_to_all | solution.py:253
  57.1 0.7 %finish.1 = (bf16[64,128]{1,0:T(8,128)(2,1)}, bf16[64,128]{1,0:T(8,128)(2,1)}, bf16[64,128]{1,0:T(8,128)(2,1)}, bf16[64,128]{1,0:T(8,128)(2,1)}, f32[32,128]{1,0:T(8,128)}) custom-call(f32[8,32,128]{2,1,0:T(8,128)S(1)} %all_to_all.17.partials_ref, bf16[64,128]{1,0:T(8,128)(2,1)S(1)} %get-tuple-element.20.refs_0_, ...), custom_call_target="tpu_custom_call" | custom-call | tf_op jit(solution)/shard_map/finish/pallas_call | solution.py:255
Async XLA Ops:
  2.2 30.6 %copy-start.2 = (bf16[256,192]{1,0:T(8,128)(2,1)S(1)}, bf16[256,192]{1,0:T(8,128)(2,1)}, u32[]{:S(2)}) copy-start(bf16[256,192]{1,0:T(8,128)(2,1)} %constant.43.clone.filter_there_ref) | copy-start | bytes 294916
  2.2 30.6 %copy-start.3 = (bf16[256,192]{1,0:T(8,128)(2,1)S(1)}, bf16[256,192]{1,0:T(8,128)(2,1)}, u32[]{:S(2)}) copy-start(bf16[256,192]{1,0:T(8,128)(2,1)} %constant.42.clone.there_ref) | copy-start | bytes 294916
  2.2 30.6 %copy-start.9 = (bf16[2,32,256]{2,1,0:T(8,128)(2,1)S(1)}, bf16[2,32,256]{2,1,0:T(8,128)(2,1)}, u32[]{:S(2)}) copy-start(bf16[2,32,256]{2,1,0:T(8,128)(2,1)} %constant.47.clone.filter_low_ref) | copy-start | bytes 98308
  2.2 30.6 %copy-start.10 = (bf16[2,32,256]{2,1,0:T(8,128)(2,1)S(1)}, bf16[2,32,256]{2,1,0:T(8,128)(2,1)}, u32[]{:S(2)}) copy-start(bf16[2,32,256]{2,1,0:T(8,128)(2,1)} %constant.46.clone.filter_high_ref) | copy-start | bytes 98308
  2.2 30.6 %copy-start.11 = (bf16[2,32,256]{2,1,0:T(8,128)(2,1)S(1)}, bf16[2,32,256]{2,1,0:T(8,128)(2,1)}, u32[]{:S(2)}) copy-start(bf16[2,32,256]{2,1,0:T(8,128)(2,1)} %constant.45.clone.low_ref) | copy-start | bytes 98308
  2.2 30.6 %copy-start.12 = (bf16[2,32,256]{2,1,0:T(8,128)(2,1)S(1)}, bf16[2,32,256]{2,1,0:T(8,128)(2,1)}, u32[]{:S(2)}) copy-start(bf16[2,32,256]{2,1,0:T(8,128)(2,1)} %constant.44.clone.high_ref) | copy-start | bytes 98308
  32.8 13.6 %copy-start.8 = (bf16[64,384]{1,0:T(8,128)(2,1)S(1)}, bf16[64,384]{1,0:T(8,128)(2,1)}, u32[]{:S(2)}) copy-start(bf16[64,384]{1,0:T(8,128)(2,1)} %constant.34.clone.pair_ref) | copy-start | bytes 147460
  32.8 13.6 %copy-start.13 = (f32[2,32,128]{2,1,0:T(8,128)S(1)}, f32[2,32,128]{2,1,0:T(8,128)}, u32[]{:S(2)}) copy-start(f32[2,32,128]{2,1,0:T(8,128)} %constant.37.clone.twiddle_ref) | copy-start | bytes 98308
  32.8 13.6 %copy-start.14 = (bf16[32,192]{1,0:T(8,128)(2,1)S(1)}, bf16[32,192]{1,0:T(8,128)(2,1)}, u32[]{:S(2)}) copy-start(bf16[32,192]{1,0:T(8,128)(2,1)} %constant.35.clone.last_ref) | copy-start | bytes 36868
  33.5 12.9 %copy-start = (bf16[256,256]{1,0:T(8,128)(2,1)S(1)}, bf16[256,256]{1,0:T(8,128)(2,1)}, u32[]{:S(2)}) copy-start(bf16[256,256]{1,0:T(8,128)(2,1)} %constant.41.clone.low_ref) | copy-start | bytes 393220
  33.6 12.9 %copy-start.1 = (bf16[256,256]{1,0:T(8,128)(2,1)S(1)}, bf16[256,256]{1,0:T(8,128)(2,1)}, u32[]{:S(2)}) copy-start(bf16[256,256]{1,0:T(8,128)(2,1)} %constant.40.clone.high_ref) | copy-start | bytes 393220
  33.6 12.9 %copy-start.4 = (bf16[2,4096]{1,0:T(2,128)(2,1)S(1)}, bf16[2,4096]{1,0:T(2,128)(2,1)}, u32[]{:S(2)}) copy-start(bf16[2,4096]{1,0:T(2,128)(2,1)} %param.23) | copy-start | bytes 49156
  33.6 12.9 %copy-start.5 = (bf16[2,4096]{1,0:T(2,128)(2,1)S(1)}, bf16[2,4096]{1,0:T(2,128)(2,1)}, u32[]{:S(2)}) copy-start(bf16[2,4096]{1,0:T(2,128)(2,1)} %param.24) | copy-start | bytes 49156
  33.6 12.9 %copy-start.6 = (bf16[2,4096]{1,0:T(2,128)(2,1)S(1)}, bf16[2,4096]{1,0:T(2,128)(2,1)}, u32[]{:S(2)}) copy-start(bf16[2,4096]{1,0:T(2,128)(2,1)} %param.27) | copy-start | bytes 49156
  33.6 12.9 %copy-start.7 = (bf16[2,4096]{1,0:T(2,128)(2,1)S(1)}, bf16[2,4096]{1,0:T(2,128)(2,1)}, u32[]{:S(2)}) copy-start(bf16[2,4096]{1,0:T(2,128)(2,1)} %param.22) | copy-start | bytes 49156

commit v10 on v8

--- a/solution.py
+++ b/solution.py
@@ -104,7 +104,7 @@
 def forward_kernel(*refs):
     operands, (out_ref, gain_ref, *held, sems) = refs[:11], refs[11:]
     copies = [pltpu.make_async_copy(src, dst, sems.at[n]) for n, (src, dst) in enumerate(zip(operands, held))]
-    for copy in copies:
+    for copy in copies[8:] + copies[:8]:
         copy.start()
     key_ref, values_ref, cot_ref, query_ref, taps_ref, pair_ref, first_ref, twiddle_ref, high_ref, low_ref, skip_ref = held
     f32 = jnp.float32

time: 58.1 us -> 58.2 us (level)
  no operation moved by 1% of the time
where the time goes in v10:
time: 58.2 us; the launch traced here: 58 us
  blocking collectives  53.5 us (92%)
  Pallas kernels  3.49 us (6%)
  between operations  0.85 us (1%)
    all_to_all x1, blocking collectives, per_device(): lax.all_to_all(sent, 'ctx', 0, 0, tiled=True, axis_index_groups=CTX_ORDER)  30.8 us
    all_to_all x1, blocking collectives, per_device(): lax.all_to_all(sent, 'ctx', 0, 0, tiled=True, axis_index_groups=HALF_ORDER)  12.6 us
    all_to_all x1, blocking collectives, per_device(): lax.all_to_all(partial_filter, 'chan', 0, 0, tiled=True, axis_index_group...  10.1 us
    pallas_call x1, Pallas kernels, per_device(): pl.pallas_call(forward_kernel, out_shape=(jax.ShapeDtypeStruct((BLOCKS, 1...  1.66 us

profile of v10, /device:TPU:1, one launch (start us, length us, event | category | flops | bytes accessed | tf_op | source)
XLA Modules:
  0.0 58.0 jit_solution(3566160176253773578)
XLA Ops:
  0.6 1.7 %forward_transform.1 = (f32[64,1,1280]{2,1,0:T(1,128)S(1)}, f32[64,128]{1,0:T(8,128)S(1)}) custom-call(bf16[64,128]{1,0:T(8,128)(2,1)} %bitcast.43, bf16[64,128]{1,0:T(8,128)(2,1)} %bitcast.45, bf16[64,128]{1,0:T(8,128)(2,1)} %bitcast.47, bf16[64,128]{1,0:T(8,128)(2,1)} %bitcast.49, f32[32,128]{1,0:T(8,128)} %bitcast.51, ...), custom_call_target="tpu_custom_call" | custom-call | tf_op jit(solution)/shard_map/forward_transform/pallas_call | solution.py:227
  2.3 0.0 copy-start.2
  2.3 0.0 copy-start.3
  2.3 0.0 copy-start.9
  2.3 0.0 copy-start.10
  2.3 0.0 copy-start.11
  2.4 0.0 copy-start.12
  2.4 30.8 %all_to_all.15.in_ref = f32[64,1,1280]{2,1,0:T(1,128)S(1)} all-to-all(f32[64,1,1280]{2,1,0:T(1,128)S(1)} %get-tuple-element.17), channel_id=1, replica_groups={{424,264,272,280,288,296,304,312,320,328,336,344,352,360,368,376,384,39..., dimensions={0} | all-to-all | bytes 655360 | tf_op jit(solution)/shard_map/all_to_all | solution.py:238
  33.2 0.0 copy-done.2
  33.2 0.0 copy-done.3
  33.2 0.0 copy-done.9
  33.2 0.0 copy-done.10
  33.2 0.0 copy-done.11
  33.2 0.0 copy-done.12
  33.2 0.0 copy-start.8
  33.3 0.0 copy-start.13
  33.3 0.0 copy-start.14
  33.3 0.7 %block_convolutions.1 = f32[32,1,1280]{2,1,0:T(1,128)S(1)} custom-call(f32[64,1,1280]{2,1,0:T(1,128)S(1)} %all_to_all.15.in_ref, bf16[256,192]{1,0:T(8,128)(2,1)S(1)} %copy-done.3, bf16[256,192]{1,0:T(8,128)(2,1)S(1)} %copy-done.2, bf16[2,32,256]{2,1,0:T(8,128)(2,1)S(1)} %copy-done.12, bf16[2,32,256]{2,1,0:T(8,128)(2,1)S(1)} %copy-done.11, ...), custom_call_target="tpu_custom_call" | custom-call | tf_op jit(solution)/shard_map/block_convolutions/pallas_call | solution.py:239
  34.0 0.0 copy-start
  34.0 0.0 copy-start.1
  34.0 0.0 copy-start.4
  34.0 0.0 copy-start.5
  34.0 0.0 copy-start.6
  34.0 0.0 copy-start.7
  34.1 12.6 %all_to_all.16.in_ref = f32[32,1,1280]{2,1,0:T(1,128)S(1)} all-to-all(f32[32,1,1280]{2,1,0:T(1,128)S(1)} %block_convolutions.1), channel_id=1, replica_groups={{160,8,16,24,32,40,48,56,64,72,80,88,96,104,112,120,128,136,144,152,0,1..., dimensions={0} | all-to-all | bytes 327680 | tf_op jit(solution)/shard_map/all_to_all | solution.py:245
  46.6 0.0 copy-done.8
  46.7 0.0 copy-done.13
  46.7 0.0 copy-done.14
  46.7 0.0 copy-done
  46.7 0.0 copy-done.1
  46.7 0.0 copy-done.4
  46.7 0.0 copy-done.5
  46.7 0.0 copy-done.6
  46.7 0.0 copy-done.7
  46.7 0.5 inverse_transform.1
  47.2 10.1 %all_to_all.17.partials_ref = f32[8,32,128]{2,1,0:T(8,128)S(1)} all-to-all(f32[8,32,128]{2,1,0:T(8,128)S(1)} %get-tuple-element.19), channel_id=1, replica_groups={{5,4,2,3,6,7,0,1},{13,12,10,11,14,15,8,9},{21,20,18,19,22,23,16,17},{29..., dimensions={0} | all-to-all | bytes 262144 | tf_op jit(solution)/shard_map/all_to_all | solution.py:253
  57.3 0.7 %finish.1 = (bf16[64,128]{1,0:T(8,128)(2,1)}, bf16[64,128]{1,0:T(8,128)(2,1)}, bf16[64,128]{1,0:T(8,128)(2,1)}, bf16[64,128]{1,0:T(8,128)(2,1)}, f32[32,128]{1,0:T(8,128)}) custom-call(f32[8,32,128]{2,1,0:T(8,128)S(1)} %all_to_all.17.partials_ref, bf16[64,128]{1,0:T(8,128)(2,1)S(1)} %get-tuple-element.20.refs_0_, ...), custom_call_target="tpu_custom_call" | custom-call | tf_op jit(solution)/shard_map/finish/pallas_call | solution.py:255
Async XLA Ops:
  2.3 30.9 %copy-start.2 = (bf16[256,192]{1,0:T(8,128)(2,1)S(1)}, bf16[256,192]{1,0:T(8,128)(2,1)}, u32[]{:S(2)}) copy-start(bf16[256,192]{1,0:T(8,128)(2,1)} %constant.43.clone.filter_there_ref) | copy-start | bytes 294916
  2.3 30.9 %copy-start.3 = (bf16[256,192]{1,0:T(8,128)(2,1)S(1)}, bf16[256,192]{1,0:T(8,128)(2,1)}, u32[]{:S(2)}) copy-start(bf16[256,192]{1,0:T(8,128)(2,1)} %constant.42.clone.there_ref) | copy-start | bytes 294916
  2.3 30.9 %copy-start.9 = (bf16[2,32,256]{2,1,0:T(8,128)(2,1)S(1)}, bf16[2,32,256]{2,1,0:T(8,128)(2,1)}, u32[]{:S(2)}) copy-start(bf16[2,32,256]{2,1,0:T(8,128)(2,1)} %constant.47.clone.filter_low_ref) | copy-start | bytes 98308
  2.3 30.9 %copy-start.10 = (bf16[2,32,256]{2,1,0:T(8,128)(2,1)S(1)}, bf16[2,32,256]{2,1,0:T(8,128)(2,1)}, u32[]{:S(2)}) copy-start(bf16[2,32,256]{2,1,0:T(8,128)(2,1)} %constant.46.clone.filter_high_ref) | copy-start | bytes 98308
  2.3 30.9 %copy-start.11 = (bf16[2,32,256]{2,1,0:T(8,128)(2,1)S(1)}, bf16[2,32,256]{2,1,0:T(8,128)(2,1)}, u32[]{:S(2)}) copy-start(bf16[2,32,256]{2,1,0:T(8,128)(2,1)} %constant.45.clone.low_ref) | copy-start | bytes 98308
  2.4 30.9 %copy-start.12 = (bf16[2,32,256]{2,1,0:T(8,128)(2,1)S(1)}, bf16[2,32,256]{2,1,0:T(8,128)(2,1)}, u32[]{:S(2)}) copy-start(bf16[2,32,256]{2,1,0:T(8,128)(2,1)} %constant.44.clone.high_ref) | copy-start | bytes 98308
  33.2 13.4 %copy-start.8 = (bf16[64,384]{1,0:T(8,128)(2,1)S(1)}, bf16[64,384]{1,0:T(8,128)(2,1)}, u32[]{:S(2)}) copy-start(bf16[64,384]{1,0:T(8,128)(2,1)} %constant.34.clone.pair_ref) | copy-start | bytes 147460
  33.3 13.4 %copy-start.13 = (f32[2,32,128]{2,1,0:T(8,128)S(1)}, f32[2,32,128]{2,1,0:T(8,128)}, u32[]{:S(2)}) copy-start(f32[2,32,128]{2,1,0:T(8,128)} %constant.37.clone.twiddle_ref) | copy-start | bytes 98308
  33.3 13.4 %copy-start.14 = (bf16[32,192]{1,0:T(8,128)(2,1)S(1)}, bf16[32,192]{1,0:T(8,128)(2,1)}, u32[]{:S(2)}) copy-start(bf16[32,192]{1,0:T(8,128)(2,1)} %constant.35.clone.last_ref) | copy-start | bytes 36868
  34.0 12.7 %copy-start = (bf16[256,256]{1,0:T(8,128)(2,1)S(1)}, bf16[256,256]{1,0:T(8,128)(2,1)}, u32[]{:S(2)}) copy-start(bf16[256,256]{1,0:T(8,128)(2,1)} %constant.41.clone.low_ref) | copy-start | bytes 393220
  34.0 12.7 %copy-start.1 = (bf16[256,256]{1,0:T(8,128)(2,1)S(1)}, bf16[256,256]{1,0:T(8,128)(2,1)}, u32[]{:S(2)}) copy-start(bf16[256,256]{1,0:T(8,128)(2,1)} %constant.40.clone.high_ref) | copy-start | bytes 393220
  34.0 12.7 %copy-start.4 = (bf16[2,4096]{1,0:T(2,128)(2,1)S(1)}, bf16[2,4096]{1,0:T(2,128)(2,1)}, u32[]{:S(2)}) copy-start(bf16[2,4096]{1,0:T(2,128)(2,1)} %param.23) | copy-start | bytes 49156
  34.0 12.7 %copy-start.5 = (bf16[2,4096]{1,0:T(2,128)(2,1)S(1)}, bf16[2,4096]{1,0:T(2,128)(2,1)}, u32[]{:S(2)}) copy-start(bf16[2,4096]{1,0:T(2,128)(2,1)} %param.24) | copy-start | bytes 49156
  34.0 12.7 %copy-start.6 = (bf16[2,4096]{1,0:T(2,128)(2,1)S(1)}, bf16[2,4096]{1,0:T(2,128)(2,1)}, u32[]{:S(2)}) copy-start(bf16[2,4096]{1,0:T(2,128)(2,1)} %param.27) | copy-start | bytes 49156
  34.0 12.7 %copy-start.7 = (bf16[2,4096]{1,0:T(2,128)(2,1)S(1)}, bf16[2,4096]{1,0:T(2,128)(2,1)}, u32[]{:S(2)}) copy-start(bf16[2,4096]{1,0:T(2,128)(2,1)} %param.22) | copy-start | bytes 49156

commit v11 on v9

--- a/solution.py
+++ b/solution.py
@@ -20,7 +20,7 @@
     return [corner if p == 0 else 0 if p == corner else p for p in range(HALVES)]
 
 
-FIRST_ORDER, SECOND_ORDER = plane_order(22), plane_order(20)
+FIRST_ORDER, SECOND_ORDER = plane_order(21), plane_order(19)
 CTX_ORDER = [[HALVES + p for p in FIRST_ORDER] + FIRST_ORDER]
 HALF_ORDER = [SECOND_ORDER, [HALVES + p for p in SECOND_ORDER]]
 CHAN_ORDER = [[5, 4, 2, 3, 6, 7, 0, 1]]

time: 58.1 us -> 60.2 us (1.036)
  blocking collectives: 53.5 us -> 55.7 us
    all_to_all x1, blocking collectives: 12.8 us -> 14.6 us  [per_device(): lax.all_to_all(sent, 'ctx', 0, 0, tiled=True, axis_index_groups=HALF_ORDER)]
where the time goes in v11:
time: 60.2 us; the launch traced here: 60 us
  blocking collectives  55.7 us (93%)
  Pallas kernels  3.36 us (6%)
  between operations  0.85 us (1%)
    all_to_all x1, blocking collectives, per_device(): lax.all_to_all(sent, 'ctx', 0, 0, tiled=True, axis_index_groups=CTX_ORDER)  30.8 us
    all_to_all x1, blocking collectives, per_device(): lax.all_to_all(sent, 'ctx', 0, 0, tiled=True, axis_index_groups=HALF_ORDER)  14.6 us
    all_to_all x1, blocking collectives, per_device(): lax.all_to_all(partial_filter, 'chan', 0, 0, tiled=True, axis_index_group...  10.2 us
    pallas_call x1, Pallas kernels, per_device(): pl.pallas_call(forward_kernel, out_shape=(jax.ShapeDtypeStruct((BLOCKS, 1...  1.52 us

profile of v11, /device:TPU:1, one launch (start us, length us, event | category | flops | bytes accessed | tf_op | source)
XLA Modules:
  0.0 60.0 jit_solution(14203128363117278083)
XLA Ops:
  0.6 1.5 %forward_transform.1 = (f32[64,1,1280]{2,1,0:T(1,128)S(1)}, f32[64,128]{1,0:T(8,128)S(1)}) custom-call(bf16[64,128]{1,0:T(8,128)(2,1)} %bitcast.43, bf16[64,128]{1,0:T(8,128)(2,1)} %bitcast.45, bf16[64,128]{1,0:T(8,128)(2,1)} %bitcast.47, bf16[64,128]{1,0:T(8,128)(2,1)} %bitcast.49, f32[32,128]{1,0:T(8,128)} %bitcast.51, ...), custom_call_target="tpu_custom_call" | custom-call | tf_op jit(solution)/shard_map/forward_transform/pallas_call | solution.py:227
  2.2 0.0 copy-start.2
  2.2 0.0 copy-start.3
  2.2 0.0 copy-start.9
  2.2 0.0 copy-start.10
  2.2 0.0 copy-start.11
  2.2 0.0 copy-start.12
  2.2 30.8 %all_to_all.15.in_ref = f32[64,1,1280]{2,1,0:T(1,128)S(1)} all-to-all(f32[64,1,1280]{2,1,0:T(1,128)S(1)} %get-tuple-element.17), channel_id=1, replica_groups={{424,264,272,280,288,296,304,312,320,328,336,344,352,360,368,376,384,39..., dimensions={0} | all-to-all | bytes 655360 | tf_op jit(solution)/shard_map/all_to_all | solution.py:238
  33.1 0.0 copy-done.2
  33.1 0.0 copy-done.3
  33.1 0.0 copy-done.9
  33.1 0.0 copy-done.10
  33.1 0.0 copy-done.11
  33.1 0.0 copy-done.12
  33.1 0.0 copy-start.8
  33.1 0.0 copy-start.13
  33.1 0.0 copy-start.14
  33.1 0.7 %block_convolutions.1 = f32[32,1,1280]{2,1,0:T(1,128)S(1)} custom-call(f32[64,1,1280]{2,1,0:T(1,128)S(1)} %all_to_all.15.in_ref, bf16[256,192]{1,0:T(8,128)(2,1)S(1)} %copy-done.3, bf16[256,192]{1,0:T(8,128)(2,1)S(1)} %copy-done.2, bf16[2,32,256]{2,1,0:T(8,128)(2,1)S(1)} %copy-done.12, bf16[2,32,256]{2,1,0:T(8,128)(2,1)S(1)} %copy-done.11, ...), custom_call_target="tpu_custom_call" | custom-call | tf_op jit(solution)/shard_map/block_convolutions/pallas_call | solution.py:239
  33.8 0.0 copy-start
  33.9 0.0 copy-start.1
  33.9 0.0 copy-start.4
  33.9 0.0 copy-start.5
  33.9 0.0 copy-start.6
  33.9 0.0 copy-start.7
  33.9 14.6 %all_to_all.16.in_ref = f32[32,1,1280]{2,1,0:T(1,128)S(1)} all-to-all(f32[32,1,1280]{2,1,0:T(1,128)S(1)} %block_convolutions.1), channel_id=1, replica_groups={{152,8,16,24,32,40,48,56,64,72,80,88,96,104,112,120,128,136,144,0,160,1..., dimensions={0} | all-to-all | bytes 327680 | tf_op jit(solution)/shard_map/all_to_all | solution.py:245
  48.6 0.0 copy-done.8
  48.6 0.0 copy-done.13
  48.6 0.0 copy-done.14
  48.6 0.0 copy-done
  48.6 0.0 copy-done.1
  48.6 0.0 copy-done.4
  48.6 0.0 copy-done.5
  48.6 0.0 copy-done.6
  48.6 0.0 copy-done.7
  48.6 0.5 inverse_transform.1
  49.1 10.2 %all_to_all.17.partials_ref = f32[8,32,128]{2,1,0:T(8,128)S(1)} all-to-all(f32[8,32,128]{2,1,0:T(8,128)S(1)} %get-tuple-element.19), channel_id=1, replica_groups={{5,4,2,3,6,7,0,1},{13,12,10,11,14,15,8,9},{21,20,18,19,22,23,16,17},{29..., dimensions={0} | all-to-all | bytes 262144 | tf_op jit(solution)/shard_map/all_to_all | solution.py:253
  59.3 0.7 %finish.1 = (bf16[64,128]{1,0:T(8,128)(2,1)}, bf16[64,128]{1,0:T(8,128)(2,1)}, bf16[64,128]{1,0:T(8,128)(2,1)}, bf16[64,128]{1,0:T(8,128)(2,1)}, f32[32,128]{1,0:T(8,128)}) custom-call(f32[8,32,128]{2,1,0:T(8,128)S(1)} %all_to_all.17.partials_ref, bf16[64,128]{1,0:T(8,128)(2,1)S(1)} %get-tuple-element.20.refs_0_, ...), custom_call_target="tpu_custom_call" | custom-call | tf_op jit(solution)/shard_map/finish/pallas_call | solution.py:255
Async XLA Ops:
  2.2 30.9 %copy-start.2 = (bf16[256,192]{1,0:T(8,128)(2,1)S(1)}, bf16[256,192]{1,0:T(8,128)(2,1)}, u32[]{:S(2)}) copy-start(bf16[256,192]{1,0:T(8,128)(2,1)} %constant.43.clone.filter_there_ref) | copy-start | bytes 294916
  2.2 30.9 %copy-start.3 = (bf16[256,192]{1,0:T(8,128)(2,1)S(1)}, bf16[256,192]{1,0:T(8,128)(2,1)}, u32[]{:S(2)}) copy-start(bf16[256,192]{1,0:T(8,128)(2,1)} %constant.42.clone.there_ref) | copy-start | bytes 294916
  2.2 30.9 %copy-start.9 = (bf16[2,32,256]{2,1,0:T(8,128)(2,1)S(1)}, bf16[2,32,256]{2,1,0:T(8,128)(2,1)}, u32[]{:S(2)}) copy-start(bf16[2,32,256]{2,1,0:T(8,128)(2,1)} %constant.47.clone.filter_low_ref) | copy-start | bytes 98308
  2.2 30.9 %copy-start.10 = (bf16[2,32,256]{2,1,0:T(8,128)(2,1)S(1)}, bf16[2,32,256]{2,1,0:T(8,128)(2,1)}, u32[]{:S(2)}) copy-start(bf16[2,32,256]{2,1,0:T(8,128)(2,1)} %constant.46.clone.filter_high_ref) | copy-start | bytes 98308
  2.2 30.9 %copy-start.11 = (bf16[2,32,256]{2,1,0:T(8,128)(2,1)S(1)}, bf16[2,32,256]{2,1,0:T(8,128)(2,1)}, u32[]{:S(2)}) copy-start(bf16[2,32,256]{2,1,0:T(8,128)(2,1)} %constant.45.clone.low_ref) | copy-start | bytes 98308
  2.2 30.9 %copy-start.12 = (bf16[2,32,256]{2,1,0:T(8,128)(2,1)S(1)}, bf16[2,32,256]{2,1,0:T(8,128)(2,1)}, u32[]{:S(2)}) copy-start(bf16[2,32,256]{2,1,0:T(8,128)(2,1)} %constant.44.clone.high_ref) | copy-start | bytes 98308
  33.1 15.5 %copy-start.8 = (bf16[64,384]{1,0:T(8,128)(2,1)S(1)}, bf16[64,384]{1,0:T(8,128)(2,1)}, u32[]{:S(2)}) copy-start(bf16[64,384]{1,0:T(8,128)(2,1)} %constant.34.clone.pair_ref) | copy-start | bytes 147460
  33.1 15.4 %copy-start.13 = (f32[2,32,128]{2,1,0:T(8,128)S(1)}, f32[2,32,128]{2,1,0:T(8,128)}, u32[]{:S(2)}) copy-start(f32[2,32,128]{2,1,0:T(8,128)} %constant.37.clone.twiddle_ref) | copy-start | bytes 98308
  33.1 15.4 %copy-start.14 = (bf16[32,192]{1,0:T(8,128)(2,1)S(1)}, bf16[32,192]{1,0:T(8,128)(2,1)}, u32[]{:S(2)}) copy-start(bf16[32,192]{1,0:T(8,128)(2,1)} %constant.35.clone.last_ref) | copy-start | bytes 36868
  33.8 14.7 %copy-start = (bf16[256,256]{1,0:T(8,128)(2,1)S(1)}, bf16[256,256]{1,0:T(8,128)(2,1)}, u32[]{:S(2)}) copy-start(bf16[256,256]{1,0:T(8,128)(2,1)} %constant.41.clone.low_ref) | copy-start | bytes 393220
  33.9 14.7 %copy-start.1 = (bf16[256,256]{1,0:T(8,128)(2,1)S(1)}, bf16[256,256]{1,0:T(8,128)(2,1)}, u32[]{:S(2)}) copy-start(bf16[256,256]{1,0:T(8,128)(2,1)} %constant.40.clone.high_ref) | copy-start | bytes 393220
  33.9 14.7 %copy-start.4 = (bf16[2,4096]{1,0:T(2,128)(2,1)S(1)}, bf16[2,4096]{1,0:T(2,128)(2,1)}, u32[]{:S(2)}) copy-start(bf16[2,4096]{1,0:T(2,128)(2,1)} %param.23) | copy-start | bytes 49156
  33.9 14.7 %copy-start.5 = (bf16[2,4096]{1,0:T(2,128)(2,1)S(1)}, bf16[2,4096]{1,0:T(2,128)(2,1)}, u32[]{:S(2)}) copy-start(bf16[2,4096]{1,0:T(2,128)(2,1)} %param.24) | copy-start | bytes 49156
  33.9 14.7 %copy-start.6 = (bf16[2,4096]{1,0:T(2,128)(2,1)S(1)}, bf16[2,4096]{1,0:T(2,128)(2,1)}, u32[]{:S(2)}) copy-start(bf16[2,4096]{1,0:T(2,128)(2,1)} %param.27) | copy-start | bytes 49156
  33.9 14.7 %copy-start.7 = (bf16[2,4096]{1,0:T(2,128)(2,1)S(1)}, bf16[2,4096]{1,0:T(2,128)(2,1)}, u32[]{:S(2)}) copy-start(bf16[2,4096]{1,0:T(2,128)(2,1)} %param.22) | copy-start | bytes 49156
